TPU v7x, 128 devices: a whole 4x4x4 slice. The times are simulated.
128 devices in a mesh: group: 8 (over x_hi, y), member: 16 (over z, x_lo, core).
Axes of the slice: x: 4 (x_hi: 2, x_lo: 2; x = x_hi * 2 + x_lo), y: 4, z: 4, core: 2. Of those that a mesh axis runs over, the one named last changes fastest.
Arguments:
- tokens: bfloat16 [16384, 2560], P(('group', 'member')), may hold values from -6 to 6
- route_ids: int32 [16384, 6], P(('group', 'member')), may hold values from 0 to 159, as said below
- route_gates: bfloat16 [16384, 6], P(('group', 'member')), may hold values from 0.099609375 to 1
- out_grad: bfloat16 [16384, 2560], P(('group', 'member')), may hold values from -6 to 6
- proj_in: float32 [2, 16, 2560, 384], P(None, 'member', 'group'), may hold values from -0.125 to 0.125
- proj_out: float32 [16, 2560, 384], P('member', 'group'), may hold values from -0.15625 to 0.15625
- first_moment: float32 [3, 16, 2560, 384], P(None, 'member', 'group'), may hold values from -12 to 12
- second_moment: float32 [3, 16, 2560, 384], P(None, 'member', 'group'), may hold values from 1 to 100
Outputs:
- layer_out: bfloat16 [16384, 2560], P(('group', 'member'))
- token_grad: bfloat16 [16384, 2560], P(('group', 'member'))
- new_proj_in: float32 [2, 16, 2560, 384], P(None, 'member', 'group')
- new_proj_out: float32 [16, 2560, 384], P('member', 'group')
- new_first: float32 [3, 16, 2560, 384], P(None, 'member', 'group')
- new_second: float32 [3, 16, 2560, 384], P(None, 'member', 'group')
Inputs may be any that keep to these rules, and one draw needn't show every extreme that they name: `route_ids`: each row names 6 different experts. Ids below 4 are the window's experts; among the rows of one device each window expert is named by at most 80 rows, and in every group one window expert is named by exactly 80 rows of each device of the group.
All inputs are finite; a program needn't handle non-finite values.
Results may differ from a plain program's by a relative error of at most 0.023.
Values may be sent and summed in bfloat16 or wider, within the bound.
A program may use at most 128 MiB of HBM per device.

v0:
```python
import jax
import jax.numpy as jnp
from jax import lax
from jax.sharding import PartitionSpec as P

SPLIT = 4
CAP = 80


beta_one = 0.9
beta_two = 0.95
learn_rate = 0.0003
decay_rate = 0.1
adam_eps = 1e-08
bias_one = 1.0 - 0.9**10
bias_two = 1.0 - 0.95**10


def route_tables(route_ids, route_gates, window):
    experts = jnp.arange(window, dtype=jnp.int32)
    hit_table = route_ids[:, :, None] == experts[None, None, :]
    matched = jnp.any(hit_table, axis=1)
    weights = jnp.sum(
        jnp.where(hit_table, route_gates[:, :, None].astype(jnp.float32), jnp.float32(0.0)), axis=1
    )
    position = jnp.cumsum(matched.astype(jnp.int32), axis=0) - 1
    return (matched, weights, position)


def collect_rows(pieces, matched, position, window, capacity):
    row_index = jnp.arange(window, dtype=jnp.int32)[None, :] * capacity + jnp.clip(
        position, 0, capacity - 1
    )
    gathered = jnp.take(pieces.reshape(window * capacity, -1), row_index, axis=0)
    return jnp.sum(jnp.where(matched[:, :, None], gathered, jnp.float32(0.0)), axis=1)


def per_device(
    tokens, route_ids, route_gates, out_grad, proj_in, proj_out, first_moment, second_moment
):
    members = lax.axis_size("member")
    window = members // SPLIT
    width = tokens.shape[1]
    capacity = CAP
    row_total = members * capacity
    pull_in, pull_out = (
        lax.all_gather(proj_in.astype(jnp.bfloat16), "group", axis=2, tiled=True),
        lax.all_gather(proj_out.astype(jnp.bfloat16), "group", axis=1, tiled=True),
    )
    w_gate = pull_in[0, 0]
    w_up = pull_in[1, 0]
    w_down = pull_out[0]
    matched, weights, position = route_tables(route_ids, route_gates, window)
    slot_axis = jnp.arange(capacity, dtype=jnp.int32)
    selector = matched.T[:, None, :] & (position.T[:, None, :] == slot_axis[None, :, None])
    select_bf = selector.astype(jnp.bfloat16)
    token_slots = jnp.einsum(
        "ect,td->ecd", select_bf, tokens, preferred_element_type=jnp.float32
    ).astype(jnp.bfloat16)
    gate_slots = jnp.sum(jnp.where(selector, weights.T[:, None, :], jnp.float32(0.0)), axis=2)
    send_rows = jnp.broadcast_to(token_slots[:, None], (window, SPLIT, capacity, width)).reshape(
        members, capacity, width
    )
    send_gates = (
        jnp.broadcast_to(gate_slots[:, None], (window, SPLIT, capacity))
        .reshape(members, capacity)
        .astype(jnp.bfloat16)
    )
    cot_slots = jnp.einsum(
        "ect,td->ecd", select_bf, out_grad, preferred_element_type=jnp.float32
    ).astype(jnp.bfloat16)
    send_cot = jnp.broadcast_to(cot_slots[:, None], (window, SPLIT, capacity, width)).reshape(
        members, capacity, width
    )
    recv_rows, recv_gates = (
        lax.all_to_all(send_rows, "member", split_axis=0, concat_axis=0, tiled=True),
        lax.all_to_all(send_gates, "member", split_axis=0, concat_axis=0, tiled=True),
    )
    slot_count = recv_rows.shape[1]
    flat_rows = recv_rows.reshape(members * slot_count, width)
    pre_gate = jnp.dot(flat_rows, w_gate, preferred_element_type=jnp.float32)
    pre_up = jnp.dot(flat_rows, w_up, preferred_element_type=jnp.float32)
    hidden = (pre_gate * jax.nn.sigmoid(pre_gate) * pre_up).astype(jnp.bfloat16)
    product = lax.dot_general(
        hidden, w_down, (((1,), (1,)), ((), ())), preferred_element_type=jnp.float32
    )
    gate_col = recv_gates.reshape(members * slot_count, 1).astype(jnp.float32)
    partial_value = (gate_col * product).astype(jnp.bfloat16).reshape(members, slot_count, width)
    partial_value, pre_gate, pre_up = (
        partial_value,
        pre_gate.reshape(members, slot_count, -1),
        pre_up.reshape(members, slot_count, -1),
    )
    returned = lax.all_to_all(partial_value, "member", split_axis=0, concat_axis=0, tiled=True)
    recv_cot = lax.all_to_all(send_cot, "member", split_axis=0, concat_axis=0, tiled=True)
    flat_rows = recv_rows.reshape(row_total, width)
    gate_col = recv_gates.reshape(row_total, 1).astype(jnp.float32)
    scaled = (gate_col * recv_cot.reshape(row_total, width)).astype(jnp.bfloat16)
    gate_flat = pre_gate.reshape(row_total, -1)
    up_flat = pre_up.reshape(row_total, -1)
    sigmoid_g = jax.nn.sigmoid(gate_flat)
    active = gate_flat * sigmoid_g
    hidden = (active * up_flat).astype(jnp.bfloat16)
    d_hidden = jnp.dot(scaled, w_down, preferred_element_type=jnp.float32)
    d_active = sigmoid_g * (1.0 + gate_flat * (1.0 - sigmoid_g))
    d_gate = (d_hidden * up_flat * d_active).astype(jnp.bfloat16)
    d_up = (d_hidden * active).astype(jnp.bfloat16)
    contract_last = (((1,), (1,)), ((), ()))
    input_part = (
        lax.dot_general(d_gate, w_gate, contract_last, preferred_element_type=jnp.float32)
        + lax.dot_general(d_up, w_up, contract_last, preferred_element_type=jnp.float32)
    ).astype(jnp.bfloat16)
    contract_first = (((0,), (0,)), ((), ()))
    grad_gate = lax.dot_general(
        flat_rows, d_gate, contract_first, preferred_element_type=jnp.float32
    )
    grad_up = lax.dot_general(flat_rows, d_up, contract_first, preferred_element_type=jnp.float32)
    grad_down = lax.dot_general(scaled, hidden, contract_first, preferred_element_type=jnp.float32)
    input_part, local_grads = (
        input_part.reshape(members, capacity, width),
        jnp.stack([grad_gate, grad_up, grad_down]),
    )
    returned_grad = lax.all_to_all(input_part, "member", split_axis=0, concat_axis=0, tiled=True)
    summed_out = jnp.sum(
        returned.reshape(window, SPLIT, capacity, width).astype(jnp.float32), axis=1
    )
    layer_out = collect_rows(summed_out, matched, position, window, capacity).astype(jnp.bfloat16)
    summed_grad = jnp.sum(
        returned_grad.reshape(window, SPLIT, capacity, width).astype(jnp.float32), axis=1
    )
    token_grad = collect_rows(summed_grad, matched, position, window, capacity).astype(jnp.bfloat16)
    gradient = lax.psum_scatter(
        local_grads.astype(jnp.bfloat16), "group", scatter_dimension=1, tiled=True
    ).astype(jnp.float32)[:, None]
    masters = jnp.concatenate([proj_in, proj_out[None]], axis=0)
    new_first = beta_one * first_moment + (1.0 - beta_one) * gradient
    new_second = beta_two * second_moment + (1.0 - beta_two) * gradient * gradient
    adam_step = (
        new_first / bias_one / (jnp.sqrt(new_second / bias_two) + adam_eps) + decay_rate * masters
    )
    updated = masters - learn_rate * adam_step
    return (layer_out, token_grad, updated[:2], updated[2], new_first, new_second)


def solution(mesh):
    return jax.shard_map(
        per_device,
        mesh=mesh,
        in_specs=(
            P(("group", "member"), None),
            P(("group", "member"), None),
            P(("group", "member"), None),
            P(("group", "member"), None),
            P(None, "member", "group", None),
            P("member", "group", None),
            P(None, "member", "group", None),
            P(None, "member", "group", None),
        ),
        out_specs=(
            P(("group", "member"), None),
            P(("group", "member"), None),
            P(None, "member", "group", None),
            P("member", "group", None),
            P(None, "member", "group", None),
            P(None, "member", "group", None),
        ),
        check_vma=False,
    )
```

profile of v0, /device:TPU:32, one launch (start us, length us, event | category | flops | bytes accessed | tf_op | source)
XLA Modules:
  0.0 491.9 jit_solution(5057737562855932470)
XLA Ops:
  7.2 0.8 fusion.30
  8.1 0.2 reduce_window_sum.11
  8.3 0.7 convert_element_type.108
  9.0 0.7 select_reduce_fusion.1
  9.7 0.1 select_reduce_fusion
  9.9 0.6 copy.69
  10.5 6.4 %all-to-all-start = ((bf16[16,1,80]{2,1,0:T(2,128)(2,1)}), bf16[16,1,80]{2,1,0:T(2,128)(2,1)S(1)}, u32[]{:S(2)}, u32[]{:S(2)}) async-start(bf16[16,1,80]{2,1,0:T(2,128)(2,1)} %copy.69), calls=%async_computation | async-start | bytes 16384 | tf_op jit(solution)/shard_map/all_to_all | solution.py:77
  16.9 0.6 convolution_convert_fusion.3
  17.4 4.0 all-to-all-done
  21.5 3.4 broadcast_in_dim.90
  24.9 6.0 %all-to-all-start.3 = ((bf16[16,80,2560]{2,1,0:T(8,128)(2,1)}), bf16[16,80,2560]{2,1,0:T(8,128)(2,1)}, u32[]{:S(2)}, u32[]{:S(2)}) async-start(bf16[16,80,2560]{2,1,0:T(8,128)(2,1)} %bitcast.108), calls=%async_computation.3 | async-start | bytes 13107200 | tf_op jit(solution)/shard_map/all_to_all | solution.py:95
  30.9 0.7 convert_element_type.116
  31.7 0.8 convert_element_type.114
  32.6 0.6 convolution_convert_fusion.4
  33.2 87.8 %all-to-all-done.3 = bf16[16,80,2560]{2,1,0:T(8,128)(2,1)} async-done(((bf16[16,80,2560]{2,1,0:T(8,128)(2,1)}), bf16[16,80,2560]{2,1,0:T(8,128)(2,1)}, u32[]{:S(2)}, u32[]{:S(2)}) %all-to-all-start.3) | async-done | bytes 6553632 | tf_op jit(solution)/shard_map/all_to_all | solution.py:95
  121.0 3.3 broadcast_in_dim.88
  124.3 5.0 %all-to-all-start.1 = ((bf16[16,80,2560]{2,1,0:T(8,128)(2,1)}), bf16[16,80,2560]{2,1,0:T(8,128)(2,1)}, u32[]{:S(2)}, u32[]{:S(2)}) async-start(bf16[16,80,2560]{2,1,0:T(8,128)(2,1)} %bitcast.109), calls=%async_computation.1 | async-start | bytes 13107200 | tf_op jit(solution)/shard_map/all_to_all | solution.py:76
  129.4 6.8 %multiply_convert_fusion = bf16[16,80,2560]{2,1,0:T(8,128)(2,1)} fusion(f32[16,80]{1,0:T(8,128)S(1)} %bitcast.114, bf16[16,80,2560]{2,1,0:T(8,128)(2,1)} %all-to-all-done.3), kind=kLoop, calls=%fused_computation.8 | loop fusion | flops 9830400 | bytes 13112320 | tf_op jit(solution)/shard_map/convert_element_type | solution.py:98
  136.2 6.3 %fusion.8 = f32[1280,384]{1,0:T(8,128)S(1)} fusion(bf16[1280,2560]{1,0:T(8,128)(2,1)} %bitcast.111, bf16[1,2560,384]{2,1,0:T(8,128)(2,1)} %all-gather.5.cloned.1.call-done), kind=kOutput, calls=%fused_computation.27 | convolution fusion | flops 2516582400 | bytes 10485760 | tf_op jit(solution)/shard_map/dot_general | solution.py:104
  142.5 6.7 %fusion = bf16[1280,2560]{1,0:T(8,128)(2,1)} fusion(f32[1280]{0:T(1024)S(1)} %reshape.140, bf16[16,80,2560]{2,1,0:T(8,128)(2,1)} %all-to-all-done.3), kind=kLoop, calls=%fused_computation.7 | loop fusion | flops 9830400 | bytes 13112320 | tf_op jit(solution)/shard_map/convert_element_type | solution.py:98
  149.2 75.1 %all-to-all-done.1 = bf16[16,80,2560]{2,1,0:T(8,128)(2,1)} async-done(((bf16[16,80,2560]{2,1,0:T(8,128)(2,1)}), bf16[16,80,2560]{2,1,0:T(8,128)(2,1)}, u32[]{:S(2)}, u32[]{:S(2)}) %all-to-all-start.1) | async-done | bytes 6553632 | tf_op jit(solution)/shard_map/all_to_all | solution.py:76
  224.3 7.4 %fusion.13 = f32[1280,384]{1,0:T(8,128)S(1)} fusion(bf16[1280,2560]{1,0:T(8,128)(2,1)} %bitcast.6, bf16[2,1,2560,384]{3,2,1,0:T(8,128)(2,1)} %all-gather.3.cloned.1.call-done), kind=kOutput, calls=%fused_computation.37 | convolution fusion | flops 2516582400 | bytes 10485760 | tf_op jit(solution)/shard_map/dot_general | solution.py:81
  231.8 8.3 %multiply_convert_fusion.3 = (bf16[1280,384]{1,0:T(8,128)(2,1)}, bf16[1280,384]{1,0:T(8,128)(2,1)S(1)}, bf16[1280,384]{1,0:T(8,128)(2,1)S(1)}) fusion(f32[1280,384]{1,0:T(8,128)S(1)} %fusion.13, f32[1280,384]{1,0:T(8,128)S(1)} %fusion.8, bf16[1280,2560]{1,0:T(8,128)(2,1)} %bitcast.6, bf16[2,1,2560,384]{3,2,1,0:T(8,128)(2,1)S(1)} %copy-done.4), kind=kOutput, calls=%fused_computation.32 | convolution fusion | flops 2523955200 | bytes 15400960 | tf_op jit(solution)/shard_map/dot_general | solution.py:82
  240.0 6.5 %fusion.5 = bf16[1,2560,384]{2,1,0:T(8,128)(2,1)S(1)} fusion(bf16[1280,2560]{1,0:T(8,128)(2,1)} %bitcast.6, bf16[1280,384]{1,0:T(8,128)(2,1)S(1)} %get-tuple-element.48), kind=kOutput, calls=%fused_computation.21 | convolution fusion | flops 2517565440 | bytes 9502720 | tf_op jit(solution)/shard_map/dot_general | solution.py:114
  246.5 3.6 fusion.12
  250.2 7.1 %fusion.1 = bf16[1280,2560]{1,0:T(8,128)(2,1)} fusion(f32[1280,2560]{1,0:T(8,128)S(1)} %fusion.12, bf16[1280,384]{1,0:T(8,128)(2,1)S(1)} %get-tuple-element.49, bf16[2,1,2560,384]{3,2,1,0:T(8,128)(2,1)} %all-gather.3.cloned.1.call-done), kind=kOutput, calls=%fused_computation.9 | convolution fusion | flops 2523136000 | bytes 22609920 | tf_op jit(solution)/shard_map/dot_general | solution.py:111
  257.2 6.3 %all-to-all-start.4 = ((bf16[16,80,2560]{2,1,0:T(8,128)(2,1)}), bf16[16,80,2560]{2,1,0:T(8,128)(2,1)}, u32[]{:S(2)}, u32[]{:S(2)}) async-start(bf16[16,80,2560]{2,1,0:T(8,128)(2,1)} %bitcast.107), calls=%async_computation.4 | async-start | bytes 13107200 | tf_op jit(solution)/shard_map/all_to_all | solution.py:123
  263.5 0.2 reduce-scatter.2.cloned.1.call-start
  263.7 6.6 %fusion.6 = bf16[1,2560,384]{2,1,0:T(8,128)(2,1)S(1)} fusion(bf16[1280,2560]{1,0:T(8,128)(2,1)} %bitcast.6, bf16[1280,384]{1,0:T(8,128)(2,1)S(1)} %get-tuple-element.49), kind=kOutput, calls=%fused_computation.22 | convolution fusion | flops 2517565440 | bytes 9502720 | tf_op jit(solution)/shard_map/dot_general | solution.py:117
  270.3 6.5 %fusion.7 = bf16[1,2560,384]{2,1,0:T(8,128)(2,1)S(1)} fusion(bf16[1280,2560]{1,0:T(8,128)(2,1)} %fusion, bf16[1280,384]{1,0:T(8,128)(2,1)S(1)} %copy-done.9), kind=kOutput, calls=%fused_computation.23 | convolution fusion | flops 2517565440 | bytes 9502720 | tf_op jit(solution)/shard_map/dot_general | solution.py:118
  276.8 3.3 pad_maximum_fusion
  280.1 1.5 copy-done.8
  281.7 0.2 copy-done.10
  281.9 5.5 %fusion.2 = bf16[1280,2560]{1,0:T(8,128)(2,1)} fusion(bf16[1280,384]{1,0:T(8,128)(2,1)S(1)} %copy-done.10, f32[1280]{0:T(1024)S(1)} %reshape.140, bf16[1,2560,384]{2,1,0:T(8,128)(2,1)S(1)} %copy-done.8), kind=kOutput, calls=%fused_computation.10 | convolution fusion | flops 2523136000 | bytes 9507840 | tf_op jit(solution)/shard_map/dot_general | solution.py:84
  287.4 73.8 %all-to-all-done.4 = bf16[16,80,2560]{2,1,0:T(8,128)(2,1)} async-done(((bf16[16,80,2560]{2,1,0:T(8,128)(2,1)}), bf16[16,80,2560]{2,1,0:T(8,128)(2,1)}, u32[]{:S(2)}, u32[]{:S(2)}) %all-to-all-start.4) | async-done | bytes 6553632 | tf_op jit(solution)/shard_map/all_to_all | solution.py:123
  361.3 6.6 %all-to-all-start.2 = ((bf16[16,80,2560]{2,1,0:T(8,128)(2,1)}), bf16[16,80,2560]{2,1,0:T(8,128)(2,1)}, u32[]{:S(2)}, u32[]{:S(2)}) async-start(bf16[16,80,2560]{2,1,0:T(8,128)(2,1)} %bitcast.110), calls=%async_computation.2 | async-start | bytes 13107200 | tf_op jit(solution)/shard_map/all_to_all | solution.py:94
  367.9 0.1 copy.65
  368.5 4.2 convert_reduce_fusion
  372.7 4.2 gather_fusion.1
  376.9 7.1 %reshape.172 = f32[128,4,2560]{2,1,0:T(4,128)} reshape(f32[512,2560]{1,0:T(8,128)} %gather_fusion.1) | data formatting | bytes 10485760 | tf_op jit(solution)/shard_map/jit(_take)/gather | solution.py:34
  384.0 66.6 %all-to-all-done.2 = bf16[16,80,2560]{2,1,0:T(8,128)(2,1)} async-done(((bf16[16,80,2560]{2,1,0:T(8,128)(2,1)}), bf16[16,80,2560]{2,1,0:T(8,128)(2,1)}, u32[]{:S(2)}, u32[]{:S(2)}) %all-to-all-start.2) | async-done | bytes 6553632 | tf_op jit(solution)/shard_map/all_to_all | solution.py:94
  450.6 4.2 convert_reduce_fusion.1
  454.8 4.0 gather_fusion
  458.9 7.1 %reshape.168 = f32[128,4,2560]{2,1,0:T(4,128)} reshape(f32[512,2560]{1,0:T(8,128)} %gather_fusion) | data formatting | bytes 10485760 | tf_op jit(solution)/shard_map/jit(_take)/gather | solution.py:34
  466.0 12.5 %fusion.3 = (bf16[128,2560]{1,0:T(8,128)(2,1)}, bf16[128,2560]{1,0:T(8,128)(2,1)}) fusion(f32[128,4,2560]{2,1,0:T(4,128)} %reshape.172, pred[128,4]{1,0:T(8,128)(4,1)S(1)} %copy.68, pred[128,4]{1,0:T(8,128)(4,1)S(1)} %copy.65, f32[128,4,2560]{2,1,0:T(4,128)} %reshape.168), kind=kLoop, calls=%fused_computation.13 | loop fusion | flops 7208960 | bytes 11797504 | tf_op jit(solution)/shard_map/reduce_sum | solution.py:35
  478.5 4.8 fusion.19
  483.3 1.0 slice_bitcast_fusion.6
  484.3 0.8 slice_bitcast_fusion.7
  (42 shorter events, 0.9 us)
Async XLA Ops:
  7.2 9.7 %copy-start = (bf16[128,2560]{1,0:T(8,128)(2,1)S(1)}, bf16[128,2560]{1,0:T(8,128)(2,1)}, u32[]{:S(2)}) copy-start(bf16[128,2560]{1,0:T(8,128)(2,1)} %param.13) | copy-start | bytes 1966084
  10.5 11.0 %all-to-all-start = ((bf16[16,1,80]{2,1,0:T(2,128)(2,1)}), bf16[16,1,80]{2,1,0:T(2,128)(2,1)S(1)}, u32[]{:S(2)}, u32[]{:S(2)}) async-start(bf16[16,1,80]{2,1,0:T(2,128)(2,1)} %copy.69), calls=%async_computation | async-start | bytes 16384 | tf_op jit(solution)/shard_map/all_to_all | solution.py:77
  24.9 6.1 %copy-start.5 = (f32[1,320,384]{2,1,0:T(8,128)S(1)}, f32[1,320,384]{2,1,0:T(8,128)}, u32[]{:S(2)}) copy-start(f32[1,320,384]{2,1,0:T(8,128)} %param.15) | copy-start | bytes 1474564
  24.9 6.9 %copy-start.2 = (f32[2,1,320,384]{3,2,1,0:T(8,128)S(1)}, f32[2,1,320,384]{3,2,1,0:T(8,128)}, u32[]{:S(2)}) copy-start(f32[2,1,320,384]{3,2,1,0:T(8,128)} %param.14) | copy-start | bytes 2949124
  24.9 96.2 %all-to-all-start.3 = ((bf16[16,80,2560]{2,1,0:T(8,128)(2,1)}), bf16[16,80,2560]{2,1,0:T(8,128)(2,1)}, u32[]{:S(2)}, u32[]{:S(2)}) async-start(bf16[16,80,2560]{2,1,0:T(8,128)(2,1)} %bitcast.108), calls=%async_computation.3 | async-start | bytes 13107200 | tf_op jit(solution)/shard_map/all_to_all | solution.py:95
  30.9 1.7 copy-start.7
  30.9 105.3 %all-gather.5.cloned.1.call-start = ((), (), s32[]{:S(2)}) async-start(), calls=%async_computation.7 | async-start | bytes 2211840 | tf_op jit(solution)/shard_map/all_gather | solution.py:48
  31.7 192.7 %all-gather.3.cloned.1.call-start = ((), (), s32[]{:S(2)}) async-start(), calls=%async_computation.6 | async-start | bytes 4423680 | tf_op jit(solution)/shard_map/all_gather | solution.py:47
  124.3 100.0 %all-to-all-start.1 = ((bf16[16,80,2560]{2,1,0:T(8,128)(2,1)}), bf16[16,80,2560]{2,1,0:T(8,128)(2,1)}, u32[]{:S(2)}, u32[]{:S(2)}) async-start(bf16[16,80,2560]{2,1,0:T(8,128)(2,1)} %bitcast.109), calls=%async_computation.1 | async-start | bytes 13107200 | tf_op jit(solution)/shard_map/all_to_all | solution.py:76
  224.3 7.4 %copy-start.4 = (bf16[2,1,2560,384]{3,2,1,0:T(8,128)(2,1)S(1)}, bf16[2,1,2560,384]{3,2,1,0:T(8,128)(2,1)}, u32[]{:S(2)}) copy-start(bf16[2,1,2560,384]{3,2,1,0:T(8,128)(2,1)} %all-gather.3.cloned.1.call-done) | copy-start | bytes 11796484
  257.2 104.0 %all-to-all-start.4 = ((bf16[16,80,2560]{2,1,0:T(8,128)(2,1)}), bf16[16,80,2560]{2,1,0:T(8,128)(2,1)}, u32[]{:S(2)}, u32[]{:S(2)}) async-start(bf16[16,80,2560]{2,1,0:T(8,128)(2,1)} %bitcast.107), calls=%async_computation.4 | async-start | bytes 13107200 | tf_op jit(solution)/shard_map/all_to_all | solution.py:123
  263.5 215.0 %reduce-scatter.2.cloned.1.call-start = ((), (), s32[]{:S(2)}) async-start(), calls=%async_computation.8 | async-start | bytes 6635520 | tf_op jit(solution)/shard_map/reduce_scatter | solution.py:132
  263.7 6.6 %copy-start.9 = (bf16[1280,384]{1,0:T(8,128)(2,1)S(1)}, bf16[1280,384]{1,0:T(8,128)(2,1)}, u32[]{:S(2)}) copy-start(bf16[1280,384]{1,0:T(8,128)(2,1)} %get-tuple-element.47) | copy-start | bytes 2949124
  280.1 1.5 copy-start.8
  280.1 1.8 copy-start.10
  361.3 89.4 %all-to-all-start.2 = ((bf16[16,80,2560]{2,1,0:T(8,128)(2,1)}), bf16[16,80,2560]{2,1,0:T(8,128)(2,1)}, u32[]{:S(2)}, u32[]{:S(2)}) async-start(bf16[16,80,2560]{2,1,0:T(8,128)(2,1)} %bitcast.110), calls=%async_computation.2 | async-start | bytes 13107200 | tf_op jit(solution)/shard_map/all_to_all | solution.py:94
  466.0 12.5 %copy-start.3 = (f32[2,1,320,384]{3,2,1,0:T(8,128)S(1)}, f32[2,1,320,384]{3,2,1,0:T(8,128)}, u32[]{:S(2)}) copy-start(f32[2,1,320,384]{3,2,1,0:T(8,128)} %param.14) | copy-start | bytes 2949124
  466.0 12.5 %copy-start.6 = (f32[1,320,384]{2,1,0:T(8,128)S(1)}, f32[1,320,384]{2,1,0:T(8,128)}, u32[]{:S(2)}) copy-start(f32[1,320,384]{2,1,0:T(8,128)} %param.15) | copy-start | bytes 1474564
  478.5 6.7 %copy-start.1 = (bf16[128,2560]{1,0:T(8,128)(2,1)S(1)}, bf16[128,2560]{1,0:T(8,128)(2,1)}, u32[]{:S(2)}) copy-start(bf16[128,2560]{1,0:T(8,128)(2,1)} %param.13) | copy-start | bytes 1966084
Sparse Core Ops, SparseCore 0:
  34.6 67.4 all-gather.4
  104.9 90.7 all-gather.2
  280.3 132.5 reduce-scatter.1
where the time goes:
time: 500 us; the launch traced here: 492 us
  waiting for transfers between devices  308 us (62%)
  matrix products  58.8 us (12%)
  other arithmetic  46.7 us (9%)
  local copies, waits for them, and re-layouts  34.1 us (7%)
  starting transfers between devices  30.5 us (6%)
  between operations  14.2 us (3%)
    all_to_all x1, waiting for transfers between devices, per_device(): lax.all_to_all(send_cot, 'member', split_axis=0, concat_axis=0, tiled=True)  87.8 us
    all_to_all x1, waiting for transfers between devices, per_device(): lax.all_to_all(send_rows, 'member', split_axis=0, concat_axis=0, tiled=True)  75.1 us
    all_to_all x1, waiting for transfers between devices, per_device(): lax.all_to_all(input_part, 'member', split_axis=0, concat_axis=0, tiled=T...  73.8 us
    all_to_all x1, waiting for transfers between devices, per_device(): lax.all_to_all(partial_value, 'member', split_axis=0, concat_axis=0, tile...  66.6 us
    gather x4, local copies, waits for them, and re-layouts, collect_rows(): jnp.take(pieces.reshape(window * capacity, -1), row_index, axis=0)  22.5 us
    convert_element_type x2, other arithmetic, per_device(): (gate_col * recv_cot.reshape(row_total, width)).astype(jnp.bfloat16)  13.5 us
    reduce_sum x1, other arithmetic, collect_rows(): jnp.sum(jnp.where(matched[:, :, None], gathered, jnp.float32(0.0)), axis=1)  12.5 us
  transfers between devices with their start and end apart: 8, of which 5 were waited for; matrix products, arithmetic and copies ran while one was open for 19% of the time, Pallas kernels for 0%

commit v1 on v0

v1 whole, which is shorter than its diff:
```python
import functools

import jax
import jax.numpy as jnp
from jax import lax
from jax.experimental import pallas as pl
from jax.experimental.pallas import tpu as pltpu
from jax.sharding import PartitionSpec as P

MESH = pl.DeviceIdType.MESH
BF = jnp.bfloat16
F32 = jnp.float32
CAP = 80
WIN = 4
TOK = 128
D = 2560
FF = 384
SH = 320
SLOTS = WIN * CAP
ROWS = 16 * CAP
HALF = 2 * CAP

beta_one = 0.9
beta_two = 0.95
learn_rate = 0.0003
decay_rate = 0.1
adam_eps = 1e-08
bias_one = 1.0 - 0.9**10
bias_two = 1.0 - 0.95**10

NN = (((1,), (0,)), ((), ()))
NT = (((1,), (1,)), ((), ()))
TN = (((0,), (0,)), ((), ()))


def dot(a, b, dims):
    return lax.dot_general(a, b, dims, preferred_element_type=F32)


def loop(count, body):
    lax.fori_loop(0, count, lambda i, c: (body(i), c)[1], 0)


def kernel(
    gates,
    tok,
    cot,
    wgu_in,
    wd_in,
    out_ref,
    tgrad_ref,
    ggu_ref,
    gd_ref,
    gates_p,
    tok_p,
    cot_p,
    slots,
    rows,
    cots,
    wgu,
    wd,
    hid,
    dgu,
    pre,
    psend,
    pown,
    precv,
    ret,
    fin_send,
    fin_recv,
    y1gu,
    y1d,
    y2gu,
    y2d,
    xgu,
    xd,
    send_sem,
    recv_sem,
    loc_sem,
    credit,
):
    g = lax.axis_index("group")
    m = lax.axis_index("member")
    xh, y = g // 4, g % 4
    z, xc = m // 4, m % 4
    x, c = xc // 2, xc % 2
    to_core = (g, z * 4 + x * 2 + (1 - c))
    to_x = (g, z * 4 + (1 - x) * 2 + c)

    def at_z(step):
        return (g, ((z + step) % 4) * 4 + xc)

    y_up, y_dn, y_far = (y + 1) % 4, (y + 3) % 4, (y + 2) % 4
    to_yup = (xh * 4 + y_up, m)
    to_ydn = (xh * 4 + y_dn, m)
    to_xh = ((1 - xh) * 4 + y, m)

    used = [0]

    def send(src, dst, target):
        i = used[0]
        used[0] += 1
        copy = pltpu.make_async_remote_copy(
            src_ref=src,
            dst_ref=dst,
            send_sem=send_sem.at[i],
            recv_sem=recv_sem.at[i],
            device_id=target,
            device_id_type=MESH,
        )
        copy.start()
        return copy

    barrier = pltpu.get_barrier_semaphore()
    for other in (to_core, to_x, at_z(1), at_z(2), at_z(3), to_yup, to_ydn, to_xh):
        pl.semaphore_signal(barrier, inc=1, device_id=other, device_id_type=MESH)
    pl.semaphore_wait(barrier, 8)

    def shard(ref, xh_, y_, first=0, count=SH):
        start = pl.multiple_of((xh_ * 4 + y_) * SH + first, 16)
        return ref.at[pl.ds(start, count)]

    def block(ref, dz, dc, dx):
        return ref.at[pl.ds(dz * SLOTS + dc * HALF + dx * CAP, CAP)]

    late = []

    c_gates = send(gates, gates_p, to_x)
    c_tok = send(tok, tok_p, to_x)
    late += [c_gates, c_tok]

    own_w = [
        pltpu.make_async_copy(wgu_in, shard(wgu, xh, y), loc_sem.at[0]),
        pltpu.make_async_copy(wd_in, shard(wd, xh, y), loc_sem.at[1]),
    ]
    for copy in own_w:
        copy.start()

    def w_first(src, buf):
        up = send(src, shard(buf, xh, y), to_yup)
        dn = send(src, shard(buf, xh, y), to_ydn)
        far = send(src, shard(buf, xh, y), to_xh)
        late.extend([up, dn, far])
        return up, dn, far

    def w_second(buf, far):
        far.wait_recv()
        part = shard(buf, 1 - xh, y)
        up = send(part, part, to_yup)
        dn = send(part, part, to_ydn)
        late.extend([up, dn])
        return up, dn

    def w_forward(buf, xh_, up, dn):
        up.wait_recv()
        part = shard(buf, xh_, y_dn, 0, SH // 2)
        on_up = send(part, part, to_yup)
        dn.wait_recv()
        part = shard(buf, xh_, y_up, SH // 2, SH // 2)
        on_dn = send(part, part, to_ydn)
        late.extend([on_up, on_dn])
        return on_up, on_dn

    gu0 = w_first(wgu_in, wgu)

    def fill(mat_ref, val_ref, dst, dx, base, gated):
        mat = mat_ref[...]
        if not gated:
            mat = jnp.where(mat > 0, jnp.ones_like(mat), jnp.zeros_like(mat))

        def tile(n):
            cols = pl.ds(pl.multiple_of(n * 512, 512), 512)
            val = dot(mat, val_ref[:, cols], NN).astype(BF)
            dst[pl.ds(dx * CAP, CAP), cols] = val[:CAP]
            slots[pl.ds(base, 3 * CAP), cols] = val[CAP:]

        loop(D // 512, tile)

    def spread(dst, dx, base):
        sent = {}
        for dz in (1, 3, 2):
            src = slots.at[pl.ds(base + (dz - 1) * CAP, CAP)]
            sent[dz] = send(src, block(dst, dz, 0, dx), at_z(4 - dz))
        return sent

    def cross(dst, dz, dx):
        copy = send(block(dst, dz, 0, dx), block(dst, dz, 1, dx), to_core)
        late.append(copy)
        return copy

    fill(gates, tok, rows, 0, 0, False)
    z_tok0 = spread(rows, 0, 0)
    core_tok, core_cot = {}, {}
    core_tok[0, 0] = cross(rows, 0, 0)

    c_gates.wait_recv()
    c_tok.wait_recv()
    fill(gates_p, tok_p, rows, 1, 3 * CAP, False)
    z_tok1 = spread(rows, 1, 3 * CAP)
    core_tok[0, 1] = cross(rows, 0, 1)
    c_cot = send(cot, cot_p, to_x)
    late.append(c_cot)

    gu1 = w_second(wgu, gu0[2])
    gu2 = w_forward(wgu, xh, gu0[0], gu0[1])
    d0 = w_first(wd_in, wd)

    for dz in (1, 3, 2):
        z_tok0[dz].wait_recv()
        core_tok[dz, 0] = cross(rows, dz, 0)
    for dz in (1, 3, 2):
        z_tok0[dz].wait_send()
    fill(gates, cot, cots, 0, 0, True)
    z_cot0 = spread(cots, 0, 0)
    core_cot[0, 0] = cross(cots, 0, 0)

    gu3 = w_forward(wgu, 1 - xh, gu1[0], gu1[1])
    d1 = w_second(wd, d0[2])
    d2 = w_forward(wd, xh, d0[0], d0[1])

    for dz in (1, 3, 2):
        z_tok1[dz].wait_recv()
        core_tok[dz, 1] = cross(rows, dz, 1)
    for dz in (1, 3, 2):
        z_tok1[dz].wait_send()
    c_cot.wait_recv()
    fill(gates_p, cot_p, cots, 1, 3 * CAP, True)
    z_cot1 = spread(cots, 1, 3 * CAP)
    core_cot[0, 1] = cross(cots, 0, 1)
    d3 = w_forward(wd, 1 - xh, d1[0], d1[1])

    for copy in gu2 + gu3:
        copy.wait_recv()
    for copy in own_w:
        copy.wait()

    def forward_one(dz):
        here = pl.ds(dz * SLOTS, SLOTS)

        def tile(n):
            cols = pl.ds(pl.multiple_of(n * 256, 256), 256)
            pre[:, cols] = dot(rows[here, :], wgu[:, cols], NN)

        loop(3, tile)

        def act(n):
            src = pl.ds(pl.multiple_of(n * 16, 16), 16)
            dst = pl.ds(pl.multiple_of(dz * SLOTS + n * 16, 16), 16)
            gate, up = pre[src, :FF], pre[src, FF:]
            sig = jax.nn.sigmoid(gate)
            active = gate * sig
            hid[dst, :] = (active * up).astype(BF)
            dgu[dst, :FF] = (up * (sig * (1.0 + gate * (1.0 - sig)))).astype(BF)
            dgu[dst, FF:] = active.astype(BF)

        loop(SLOTS // 16, act)

    def core_wait(table, dz):
        table[dz, 0].wait_recv()
        table[dz, 1].wait_recv()

    for dz in (0, 1, 3, 2):
        core_wait(core_tok, dz)
        forward_one(dz)
        if dz == 1:
            for step in (1, 3, 2):
                z_cot0[step].wait_recv()
                core_cot[step, 0] = cross(cots, step, 0)

    for copy in d2 + d3:
        copy.wait_recv()

    def product(left, right, dz, arr):
        here = pl.ds(dz * SLOTS, SLOTS)

        def tile(n):
            cols = pl.ds(pl.multiple_of(n * 256, 256), 256)
            val = dot(left[here, :], right[cols, :], NT).astype(BF)
            pown[pl.ds((arr * 4 + dz) * HALF, HALF), cols] = val[:HALF]
            psend[pl.ds(dz * HALF, HALF), cols] = val[HALF:]

        loop(D // 256, tile)

    def hand_over(dz):
        part = pl.ds(dz * HALF, HALF)
        return send(psend.at[part], precv.at[part], to_core)

    def add_up(dz, arr, copy):
        copy.wait_recv()

        def tile(n):
            k = pl.multiple_of(n * 16, 16)
            a = pown[pl.ds((arr * 4 + dz) * HALF + k, 16), :].astype(F32)
            b = precv[pl.ds(dz * HALF + k, 16), :].astype(F32)
            pown[pl.ds((arr * 4 + dz) * HALF + k, 16), :] = (a + b).astype(BF)

        loop(HALF // 16, tile)

    def give_back(dz, arr):
        got = []
        for dx in (0, 1):
            src = pown.at[pl.ds((arr * 4 + dz) * HALF + dx * CAP, CAP)]
            dst = ret.at[pl.ds((arr * 2 + dx) * SLOTS + dz * CAP, CAP)]
            if dz == 0:
                copy = pltpu.make_async_copy(src, dst, loc_sem.at[2 + arr * 2 + dx])
                copy.start()
            else:
                copy = send(src, dst, at_z(dz))
                late.append(copy)
            got.append(copy)
        return got

    order = (1, 3, 2, 0)
    hand = {}
    back = {}
    for dz in order:
        product(hid, wd, dz, 0)
        hand[dz] = hand_over(dz)
    for dz in order:
        add_up(dz, 0, hand[dz])
        pl.semaphore_signal(credit.at[dz], inc=1, device_id=to_core, device_id_type=MESH)
        back[0, dz] = give_back(dz, 0)

    for dz in (1, 3, 2):
        z_cot1[dz].wait_recv()
        core_cot[dz, 1] = cross(cots, dz, 1)

    def backward_one(dz):
        here = pl.ds(dz * SLOTS, SLOTS)
        pre[:, :FF] = dot(cots[here, :], wd[...], NN)

        def act(n):
            src = pl.ds(pl.multiple_of(n * 16, 16), 16)
            dst = pl.ds(pl.multiple_of(dz * SLOTS + n * 16, 16), 16)
            dh = pre[src, :FF]
            dgu[dst, :FF] = (dgu[dst, :FF].astype(F32) * dh).astype(BF)
            dgu[dst, FF:] = (dgu[dst, FF:].astype(F32) * dh).astype(BF)

        loop(SLOTS // 16, act)

    hand_b = {}
    for dz in order:
        core_wait(core_cot, dz)
        backward_one(dz)
        hand[dz].wait_send()
        pl.semaphore_wait(credit.at[dz], 1)
        product(dgu, wgu, dz, 1)
        hand_b[dz] = hand_over(dz)
    for dz in order:
        add_up(dz, 1, hand_b[dz])
        back[1, dz] = give_back(dz, 1)

    for copy in late:
        copy.wait_send()
    done = len(late)

    def weight_grad(xh_, pair):
        cols = pl.ds(pl.multiple_of((xh_ * 2 + pair) * 2 * SH, 128), 2 * SH)
        where = pl.ds(pl.multiple_of((xh_ * 2 + pair) * 2 * SH, 128), 2 * SH)
        wgu[where, :] = dot(rows[:, cols], dgu[...], TN).astype(BF)
        wd[where, :] = dot(cots[:, cols], hid[...], TN).astype(BF)

    near = y // 2
    loop(2, lambda i: weight_grad(i, 1 - near))
    first = []
    for xh_ in (0, 1):
        for buf, land in ((wgu, y1gu), (wd, y1d)):
            part = shard(buf, xh_, y_far, 0, SH // 2)
            up = send(part, land.at[xh_], to_yup)
            part = shard(buf, xh_, y_far, SH // 2, SH // 2)
            dn = send(part, land.at[2 + xh_], to_ydn)
            late += [up, dn]
            first.append((xh_, buf, land, up, dn))
    loop(2, lambda i: weight_grad(i, near))

    def add_into(buf, start, land, k):
        def tile(n):
            r = pl.multiple_of(n * 16, 16)
            at = pl.ds(pl.multiple_of(start + r, 16), 16)
            a = buf[at, :].astype(F32) + land[k, pl.ds(r, 16), :].astype(F32)
            buf[at, :] = a.astype(BF)

        loop(SH // 2 // 16, tile)

    second = []
    for xh_, buf, land, up, dn in first:
        land2 = y2gu if buf is wgu else y2d
        up.wait_recv()
        add_into(buf, (xh_ * 4 + y_up) * SH, land, xh_)
        on_up = send(shard(buf, xh_, y_up), land2.at[xh_], to_yup)
        dn.wait_recv()
        add_into(buf, (xh_ * 4 + y_dn) * SH + SH // 2, land, 2 + xh_)
        on_dn = send(shard(buf, xh_, y_dn), land2.at[2 + xh_], to_ydn)
        late += [on_up, on_dn]
        second += [on_up, on_dn]

    def combine(arr):
        for copy in back[arr, 0]:
            copy.wait()
        for dz in (1, 3, 2):
            for copy in back[arr, dz]:
                copy.wait_recv()

        def pick(mat):
            if arr == 1:
                mat = jnp.where(mat > 0, jnp.ones_like(mat), jnp.zeros_like(mat))
            return mat

        mat_p = pick(gates_p[...])

        def tile(n):
            cols = pl.ds(pl.multiple_of(n * 512, 512), 512)
            part = ret[pl.ds((arr * 2 + 1) * SLOTS, SLOTS), cols]
            fin_send[arr, :, cols] = dot(mat_p, part, TN).astype(BF)

        loop(D // 512, tile)
        copy = send(fin_send.at[arr], fin_recv.at[arr], to_x)
        late.append(copy)
        return copy, pick(gates[...])

    def finish(arr, copy, mat, dst):
        copy.wait_recv()

        def tile(n):
            cols = pl.ds(pl.multiple_of(n * 512, 512), 512)
            part = ret[pl.ds(arr * 2 * SLOTS, SLOTS), cols]
            total = dot(mat, part, TN) + fin_recv[arr, :, cols].astype(F32)
            dst[:, cols] = total.astype(BF)

        loop(D // 512, tile)

    comb0 = combine(0)

    for copy in second:
        copy.wait_recv()

    def owner_sum(xh_, buf, land):
        start = (xh_ * 4 + y) * SH

        def value(r):
            at = pl.ds(pl.multiple_of(start + r, 16), 16)
            here = pl.ds(r, 16)
            total = buf[at, :].astype(F32) + land[xh_, here, :].astype(F32)
            return total + land[2 + xh_, here, :].astype(F32)

        return start, value

    last = []
    for buf, land, out, recv in ((wgu, y2gu, ggu_ref, xgu), (wd, y2d, gd_ref, xd)):
        start, value = owner_sum(1 - xh, buf, land)

        def tile(n, buf=buf, start=start, value=value):
            r = pl.multiple_of(n * 16, 16)
            buf[pl.ds(pl.multiple_of(start + r, 16), 16), :] = value(r).astype(BF)

        loop(SH // 16, tile)
        copy = send(shard(buf, 1 - xh, y), recv, to_xh)
        late.append(copy)
        last.append(copy)
    finish(0, *comb0, out_ref)
    comb1 = combine(1)
    for copy, (buf, land, out, recv) in zip(
        last, ((wgu, y2gu, ggu_ref, xgu), (wd, y2d, gd_ref, xd))
    ):
        copy.wait_recv()
        start, value = owner_sum(xh, buf, land)

        def tile(n, out=out, value=value, recv=recv):
            r = pl.multiple_of(n * 16, 16)
            out[pl.ds(r, 16), :] = value(r) + recv[pl.ds(r, 16), :].astype(F32)

        loop(SH // 16, tile)
    finish(1, *comb1, tgrad_ref)

    for copy in late[done:]:
        copy.wait_send()
    for copies in (z_cot0, z_cot1):
        for copy in copies.values():
            copy.wait_send()
    for dz in order:
        hand_b[dz].wait_send()
    assert used[0] <= N_COPY, used[0]


N_COPY = 128


def exchange(gates, tok, cot, wgu, wd):
    vmem = pl.BlockSpec(memory_space=pltpu.VMEM)
    shapes = [
        jax.ShapeDtypeStruct((TOK, D), BF),
        jax.ShapeDtypeStruct((TOK, D), BF),
        jax.ShapeDtypeStruct((SH, 2 * FF), F32),
        jax.ShapeDtypeStruct((SH, FF), F32),
    ]
    scratch = [
        pltpu.VMEM((SLOTS, TOK), BF),
        pltpu.VMEM((TOK, D), BF),
        pltpu.VMEM((TOK, D), BF),
        pltpu.VMEM((6 * CAP, D), BF),
        pltpu.VMEM((ROWS, D), BF),
        pltpu.VMEM((ROWS, D), BF),
        pltpu.VMEM((D, 2 * FF), BF),
        pltpu.VMEM((D, FF), BF),
        pltpu.VMEM((ROWS, FF), BF),
        pltpu.VMEM((ROWS, 2 * FF), BF),
        pltpu.VMEM((SLOTS, 2 * FF), F32),
        pltpu.VMEM((4 * HALF, D), BF),
        pltpu.VMEM((8 * HALF, D), BF),
        pltpu.VMEM((4 * HALF, D), BF),
        pltpu.VMEM((4 * SLOTS, D), BF),
        pltpu.VMEM((2, TOK, D), BF),
        pltpu.VMEM((2, TOK, D), BF),
        pltpu.VMEM((4, SH // 2, 2 * FF), BF),
        pltpu.VMEM((4, SH // 2, FF), BF),
        pltpu.VMEM((4, SH, 2 * FF), BF),
        pltpu.VMEM((4, SH, FF), BF),
        pltpu.VMEM((SH, 2 * FF), BF),
        pltpu.VMEM((SH, FF), BF),
        pltpu.SemaphoreType.DMA((N_COPY,)),
        pltpu.SemaphoreType.DMA((N_COPY,)),
        pltpu.SemaphoreType.DMA((6,)),
        pltpu.SemaphoreType.REGULAR((4,)),
    ]
    return pl.pallas_call(
        kernel,
        out_shape=shapes,
        in_specs=[vmem] * 5,
        out_specs=[vmem] * 4,
        scratch_shapes=scratch,
        compiler_params=pltpu.CompilerParams(
            collective_id=0, has_side_effects=True, vmem_limit_bytes=65 * 2**20 - 2**20
        ),
        cost_estimate=pl.CostEstimate(
            flops=18 * ROWS * D * FF, bytes_accessed=2**22, transcendentals=ROWS * FF
        ),
        name="experts",
    )(gates, tok, cot, wgu, wd)


def slot_gates(route_ids, route_gates):
    z = lax.axis_index("member") // 4
    experts = (z - jnp.arange(WIN, dtype=jnp.int32)) % WIN
    hit = route_ids[:, :, None] == experts[None, None, :]
    matched = jnp.any(hit, axis=1)
    weight = jnp.sum(jnp.where(hit, route_gates[:, :, None].astype(F32), 0.0), axis=1)
    position = jnp.cumsum(matched.astype(jnp.int32), axis=0) - 1
    slot = jnp.arange(CAP, dtype=jnp.int32)
    chosen = matched.T[:, None, :] & (position.T[:, None, :] == slot[None, :, None])
    return jnp.where(chosen, weight.T[:, None, :], 0.0).astype(BF).reshape(SLOTS, TOK)


def per_device(
    tokens, route_ids, route_gates, out_grad, proj_in, proj_out, first_moment, second_moment
):
    gates = slot_gates(route_ids, route_gates)
    wgu = jnp.concatenate([proj_in[0, 0], proj_in[1, 0]], axis=1).astype(BF)
    wd = proj_out[0].astype(BF)
    layer_out, token_grad, ggu, gd = exchange(gates, tokens, out_grad, wgu, wd)
    gradient = jnp.stack([ggu[:, :FF], ggu[:, FF:], gd])[:, None]
    masters = jnp.concatenate([proj_in, proj_out[None]], axis=0)
    new_first = beta_one * first_moment + (1.0 - beta_one) * gradient
    new_second = beta_two * second_moment + (1.0 - beta_two) * gradient * gradient
    adam_step = (
        new_first / bias_one / (jnp.sqrt(new_second / bias_two) + adam_eps) + decay_rate * masters
    )
    updated = masters - learn_rate * adam_step
    return (layer_out, token_grad, updated[:2], updated[2], new_first, new_second)


def solution(mesh):
    rows = P(("group", "member"), None)
    return jax.shard_map(
        per_device,
        mesh=mesh,
        in_specs=(
            rows,
            rows,
            rows,
            rows,
            P(None, "member", "group", None),
            P("member", "group", None),
            P(None, "member", "group", None),
            P(None, "member", "group", None),
        ),
        out_specs=(
            rows,
            rows,
            P(None, "member", "group", None),
            P("member", "group", None),
            P(None, "member", "group", None),
            P(None, "member", "group", None),
        ),
        check_vma=False,
    )
```

time: 500 us -> 257 us (0.51); the launches traced: 492 us -> 257 us
  waiting for transfers between devices: 308 us -> 0 us
  Pallas kernels: 0 us -> 240 us
  matrix products: 58.8 us -> 0 us
  other arithmetic: 46.7 us -> 10.5 us
  starting transfers between devices: 30.5 us -> 0 us
  local copies, waits for them, and re-layouts: 34.1 us -> 5.56 us
  between operations: 14.2 us -> 0.72 us
    all_to_all x5 -> x0, waiting for transfers between devices: 307 us -> none  [the longest x1 87.8 us: per_device(): lax.all_to_all(send_cot, 'member', split_axis=0, concat_axis=0, tiled=True)]
    pallas_call x0 -> x1, Pallas kernels: none -> 240 us  [exchange(): pl.pallas_call(kernel, out_shape=shapes, in_specs=[vmem] * 5, out_specs=[...]
    dot_general x11 -> x0, matrix products: 58.8 us -> none  [the longest x1 8.27 us: per_device(): pre_up = jnp.dot(flat_rows, w_up, preferred_element_type=jnp.float32)]
    all_to_all x5 -> x0, starting transfers between devices: 30.3 us -> none  [the longest x1 6.63 us: per_device(): lax.all_to_all(partial_value, 'member', split_axis=0, concat_axis=0, tile...]
    gather x4 -> x0, local copies, waits for them, and re-layouts: 22.5 us -> none  [collect_rows(): jnp.take(pieces.reshape(window * capacity, -1), row_index, axis=0)]
    reduce_sum x5 -> x1, other arithmetic: 21.7 us -> 0.77 us  [slot_gates(): jnp.sum(jnp.where(hit, route_gates[:, :, None].astype(F32), 0.0), axis=1)]
    convert_element_type x8 -> x4, other arithmetic: 15.8 us -> 3.21 us  [the longest x1 1.75 us: per_device(): wd = proj_out[0].astype(BF)]
    broadcast_in_dim x4 -> x0, local copies, waits for them, and re-layouts: 6.79 us -> none  [the longest x1 3.38 us: per_device(): jnp.broadcast_to(cot_slots[:, None], (window, SPLIT, capacity, width))]
  transfers between devices with their start and end apart: 8 -> 0, of which waited for: 5 -> 0; matrix products, arithmetic and copies ran while one was open for 19% -> 0% of each run, Pallas kernels for 0% -> 0%
where the time goes in v1:
time: 257 us
  Pallas kernels  240 us (93%)
  other arithmetic  10.5 us (4%)
  local copies, waits for them, and re-layouts  5.56 us (2%)
    pallas_call x1, Pallas kernels, exchange(): pl.pallas_call(kernel, out_shape=shapes, in_specs=[vmem] * 5, out_specs=[...  240 us

profile of v1, /device:TPU:32, one launch (start us, length us, event | category | flops | bytes accessed | tf_op | source)
XLA Modules:
  0.0 257.1 jit_solution(17844879540428667711)
XLA Ops:
  0.6 0.0 copy-start
  0.7 0.9 compare_reduce_fusion
  1.5 0.1 eq.41
  1.6 0.7 convert_element_type.18
  2.3 0.8 fusion.3
  3.1 0.1 copy.18
  3.2 0.2 reduce_window_sum.11
  3.4 0.1 copy.19
  3.4 0.8 fusion.1.gates
  4.2 1.8 convert_bitcast_fusion.wd_in
  6.0 0.0 copy-done
  6.0 0.1 convert.8
  6.0 0.1 slice_bitcast_fusion.4
  6.1 0.8 pad_maximum_fusion.2.wgu_in
  6.9 240.4 %experts.1 = (bf16[128,2560]{1,0:T(8,128)(2,1)}, bf16[128,2560]{1,0:T(8,128)(2,1)}, f32[320,768]{1,0:T(8,128)}, f32[320,384]{1,0:T(8,128)}) custom-call(bf16[320,128]{1,0:T(8,128)(2,1)} %fusion.1.gates, bf16[128,2560]{1,0:T(8,128)(2,1)} %tok.1, bf16[128,2560]{1,0:T(8,128)(2,1)} %cot.1, bf16[320,768]{1,0:T(8,128)(2,1)} %pad_maximum_fusion.2.wgu_in, ...), custom_call_target="tpu_custom_call" | custom-call | flops 22649241600 | bytes 4194304 | tf_op jit(solution)/shard_map/experts/pallas_call | solution.py:525
  247.3 0.0 copy-start.1
  247.3 0.0 copy-start.2
  247.3 0.0 copy-start.5
  247.3 1.4 slice_bitcast_fusion.2
  248.7 0.1 copy-done.1
  248.8 0.1 copy-done.2
  248.9 0.1 copy-done.5
  249.1 4.6 %multiply_subtract_fusion = (f32[3,1,320,384]{3,2,1,0:T(8,128)S(1)}, f32[3,1,320,384]{3,2,1,0:T(8,128)}, f32[3,1,320,384]{3,2,1,0:T(8,128)}) fusion(f32[1,1,320,384]{3,2,1,0:T(8,128)S(1)} %bitcast.30, f32[2,1,320,384]{3,2,1,0:T(8,128)S(1)} %copy-done.1, f32[1,1,320,384]{3,2,1,0:T(8,128)S(1)} %bitcast.31, f32[1,1,320,384]{3,2,1,0:T(8,128)S(1)} %get-tuple-element.18, ...), kind=kLoop, calls=%fused_computation.4 | loop fusion | flops 6635520 | bytes 10321920 | tf_op jit(solution)/shard_map/sub | solution.py:567
  253.6 0.0 copy-start.4
  253.6 0.8 slice_bitcast_fusion
  254.5 0.0 copy-start.3
  254.5 1.0 slice.28
  255.5 0.0 copy-done.4
  255.5 0.8 copy.22
  256.3 0.0 copy-done.3
  256.3 0.8 copy.23
  (4 shorter events, 0.0 us)
Async XLA Ops:
  0.6 5.3 %copy-start = (f32[2,1,320,384]{3,2,1,0:T(8,128)S(1)}, f32[2,1,320,384]{3,2,1,0:T(8,128)}, u32[]{:S(2)}) copy-start(f32[2,1,320,384]{3,2,1,0:T(8,128)} %param.12) | copy-start | bytes 2949124
  247.3 1.5 copy-start.1
  247.3 1.6 copy-start.2
  247.3 1.7 copy-start.5
  253.6 1.8 copy-start.4
  254.5 1.9 copy-start.3

commit v2 on v1

--- a/solution.py
+++ b/solution.py
@@ -19,6 +19,9 @@
 SLOTS = WIN * CAP
 ROWS = 16 * CAP
 HALF = 2 * CAP
+CA = 1792
+CB = D - CA
+A, B = pl.ds(0, CA), pl.ds(CA, CB)
 
 beta_one = 0.9
 beta_two = 0.95
@@ -68,6 +71,7 @@
     ret,
     fin_send,
     fin_recv,
+    xret,
     y1gu,
     y1d,
     y2gu,
@@ -126,7 +130,7 @@
     late = []
 
     c_gates = send(gates, gates_p, to_x)
-    c_tok = send(tok, tok_p, to_x)
+    c_tok = send(tok.at[:, A], tok_p, to_x)
     late += [c_gates, c_tok]
 
     own_w = [
@@ -136,98 +140,117 @@
     for copy in own_w:
         copy.start()
 
+    w_sent = []
+
     def w_first(src, buf):
         up = send(src, shard(buf, xh, y), to_yup)
         dn = send(src, shard(buf, xh, y), to_ydn)
+        late.extend([up, dn])
+        return up, dn
+
+    def w_far(src, buf):
         far = send(src, shard(buf, xh, y), to_xh)
-        late.extend([up, dn, far])
-        return up, dn, far
+        late.append(far)
+        return far
 
     def w_second(buf, far):
         far.wait_recv()
         part = shard(buf, 1 - xh, y)
         up = send(part, part, to_yup)
         dn = send(part, part, to_ydn)
-        late.extend([up, dn])
+        w_sent.extend([up, dn])
         return up, dn
 
-    def w_forward(buf, xh_, up, dn):
+    def w_forward(buf, xh_, pair):
+        up, dn = pair
         up.wait_recv()
         part = shard(buf, xh_, y_dn, 0, SH // 2)
         on_up = send(part, part, to_yup)
         dn.wait_recv()
         part = shard(buf, xh_, y_up, SH // 2, SH // 2)
         on_dn = send(part, part, to_ydn)
-        late.extend([on_up, on_dn])
+        w_sent.extend([on_up, on_dn])
         return on_up, on_dn
 
     gu0 = w_first(wgu_in, wgu)
-
-    def fill(mat_ref, val_ref, dst, dx, base, gated):
+    gu_far = w_far(wgu_in, wgu)
+    d0 = w_first(wd_in, wd)
+
+    def fill(mat_ref, val_ref, dst, dx, base, gated, width, step):
         mat = mat_ref[...]
         if not gated:
             mat = jnp.where(mat > 0, jnp.ones_like(mat), jnp.zeros_like(mat))
 
         def tile(n):
-            cols = pl.ds(pl.multiple_of(n * 512, 512), 512)
+            cols = pl.ds(pl.multiple_of(n * step, 128), step)
             val = dot(mat, val_ref[:, cols], NN).astype(BF)
             dst[pl.ds(dx * CAP, CAP), cols] = val[:CAP]
-            slots[pl.ds(base, 3 * CAP), cols] = val[CAP:]
-
-        loop(D // 512, tile)
-
-    def spread(dst, dx, base):
-        sent = {}
-        for dz in (1, 3, 2):
-            src = slots.at[pl.ds(base + (dz - 1) * CAP, CAP)]
-            sent[dz] = send(src, block(dst, dz, 0, dx), at_z(4 - dz))
-        return sent
-
-    def cross(dst, dz, dx):
-        copy = send(block(dst, dz, 0, dx), block(dst, dz, 1, dx), to_core)
+            slots[pl.ds(base * 3 * CAP, 3 * CAP), cols] = val[CAP:]
+
+        loop(width // step, tile)
+
+    def spread(dst, dx, base, dz):
+        src = slots.at[pl.ds((base * 3 + dz - 1) * CAP, CAP)]
+        land = block(dst, dz, 0, dx)
+        if dx == 1:
+            src, land = src.at[:, A], land.at[:, A]
+        copy = send(src, land, at_z(4 - dz))
         late.append(copy)
         return copy
 
-    fill(gates, tok, rows, 0, 0, False)
-    z_tok0 = spread(rows, 0, 0)
+    def cross(dst, dz, dx, cols):
+        copy = send(
+            block(dst, dz, 0, dx).at[:, cols], block(dst, dz, 1, dx).at[:, cols], to_core
+        )
+        late.append(copy)
+        return copy
+
+    def own_in(dst, table, dz):
+        table[dz, 0] = cross(dst, dz, 0, pl.ds(0, D))
+        copy = send(block(dst, dz, 0, 0).at[:, B], block(dst, dz, 0, 1).at[:, B], to_x)
+        late.append(copy)
+        table[dz, "x"] = copy
+
+    def last_in(dst, table, dz):
+        table[dz, "x"].wait_recv()
+        table[dz, 2] = cross(dst, dz, 1, B)
+
     core_tok, core_cot = {}, {}
-    core_tok[0, 0] = cross(rows, 0, 0)
+    fill(gates, tok, rows, 0, 0, False, D, 512)
+    z_tok0 = {dz: spread(rows, 0, 0, dz) for dz in (1, 3, 2)}
+    own_in(rows, core_tok, 0)
+    fill(gates, cot, cots, 0, 2, True, D, 512)
+    gu2 = w_forward(wgu, xh, gu0)
+    d2 = w_forward(wd, xh, d0)
 
     c_gates.wait_recv()
     c_tok.wait_recv()
-    fill(gates_p, tok_p, rows, 1, 3 * CAP, False)
-    z_tok1 = spread(rows, 1, 3 * CAP)
-    core_tok[0, 1] = cross(rows, 0, 1)
-    c_cot = send(cot, cot_p, to_x)
-    late.append(c_cot)
-
-    gu1 = w_second(wgu, gu0[2])
-    gu2 = w_forward(wgu, xh, gu0[0], gu0[1])
-    d0 = w_first(wd_in, wd)
-
+    fill(gates_p, tok_p, rows, 1, 1, False, CA, 896)
+    z_tok1 = {dz: spread(rows, 1, 1, dz) for dz in (1, 3, 2)}
+    core_tok[0, 1] = cross(rows, 0, 1, A)
     for dz in (1, 3, 2):
         z_tok0[dz].wait_recv()
-        core_tok[dz, 0] = cross(rows, dz, 0)
-    for dz in (1, 3, 2):
-        z_tok0[dz].wait_send()
-    fill(gates, cot, cots, 0, 0, True)
-    z_cot0 = spread(cots, 0, 0)
-    core_cot[0, 0] = cross(cots, 0, 0)
-
-    gu3 = w_forward(wgu, 1 - xh, gu1[0], gu1[1])
-    d1 = w_second(wd, d0[2])
-    d2 = w_forward(wd, xh, d0[0], d0[1])
-
+        own_in(rows, core_tok, dz)
+    c_cot = send(cot.at[:, A], cot_p, to_x)
+    late.append(c_cot)
+    d_far = w_far(wd_in, wd)
+    z_cot0 = {dz: spread(cots, 0, 2, dz) for dz in (1, 3)}
+    gu1 = w_second(wgu, gu_far)
+    z_cot0[2] = spread(cots, 0, 2, 2)
+    last_in(rows, core_tok, 0)
+    own_in(cots, core_cot, 0)
     for dz in (1, 3, 2):
         z_tok1[dz].wait_recv()
-        core_tok[dz, 1] = cross(rows, dz, 1)
-    for dz in (1, 3, 2):
-        z_tok1[dz].wait_send()
+        core_tok[dz, 1] = cross(rows, dz, 1, A)
+        last_in(rows, core_tok, dz)
     c_cot.wait_recv()
-    fill(gates_p, cot_p, cots, 1, 3 * CAP, True)
-    z_cot1 = spread(cots, 1, 3 * CAP)
-    core_cot[0, 1] = cross(cots, 0, 1)
-    d3 = w_forward(wd, 1 - xh, d1[0], d1[1])
+    fill(gates_p, cot_p, cots, 1, 3, True, CA, 896)
+    z_cot1 = {dz: spread(cots, 1, 3, dz) for dz in (1, 3)}
+    core_cot[0, 1] = cross(cots, 0, 1, A)
+    gu3 = w_forward(wgu, 1 - xh, gu1)
+    d1 = w_second(wd, d_far)
+    z_cot1[2] = spread(cots, 1, 3, 2)
+    last_in(cots, core_cot, 0)
 
     for copy in gu2 + gu3:
         copy.wait_recv()
@@ -256,16 +279,30 @@
         loop(SLOTS // 16, act)
 
     def core_wait(table, dz):
-        table[dz, 0].wait_recv()
-        table[dz, 1].wait_recv()
-
-    for dz in (0, 1, 3, 2):
-        core_wait(core_tok, dz)
-        forward_one(dz)
-        if dz == 1:
-            for step in (1, 3, 2):
-                z_cot0[step].wait_recv()
-                core_cot[step, 0] = cross(cots, step, 0)
+        for part in range(3):
+            table[dz, part].wait_recv()
+
+    def cot_one(dz):
+        z_cot0[dz].wait_recv()
+        own_in(cots, core_cot, dz)
+
+    def cot_two(dz):
+        z_cot1[dz].wait_recv()
+        core_cot[dz, 1] = cross(cots, dz, 1, A)
+        last_in(cots, core_cot, dz)
+
+    core_wait(core_tok, 0)
+    forward_one(0)
+    d3 = w_forward(wd, 1 - xh, d1)
+    core_wait(core_tok, 1)
+    forward_one(1)
+    cot_one(1)
+    cot_one(3)
+    core_wait(core_tok, 3)
+    forward_one(3)
+    cot_one(2)
+    core_wait(core_tok, 2)
+    forward_one(2)
 
     for copy in d2 + d3:
         copy.wait_recv()
@@ -274,12 +311,12 @@
         here = pl.ds(dz * SLOTS, SLOTS)
 
         def tile(n):
-            cols = pl.ds(pl.multiple_of(n * 256, 256), 256)
+            cols = pl.ds(pl.multiple_of(n * 512, 512), 512)
             val = dot(left[here, :], right[cols, :], NT).astype(BF)
             pown[pl.ds((arr * 4 + dz) * HALF, HALF), cols] = val[:HALF]
             psend[pl.ds(dz * HALF, HALF), cols] = val[HALF:]
 
-        loop(D // 256, tile)
+        loop(D // 512, tile)
 
     def hand_over(dz):
         part = pl.ds(dz * HALF, HALF)
@@ -296,36 +333,51 @@
 
         loop(HALF // 16, tile)
 
+    def swap(dz, arr):
+        src = pown.at[pl.ds((arr * 4 + dz) * HALF + CAP, CAP), B]
+        copy = send(src, xret.at[pl.ds((arr * 4 + dz) * CAP, CAP)], to_x)
+        late.append(copy)
+        swapped[arr, dz] = copy
+
+    def add_swapped(dz, arr):
+        swapped[arr, dz].wait_recv()
+        a = pown[pl.ds((arr * 4 + dz) * HALF, CAP), CA:].astype(F32)
+        b = xret[pl.ds((arr * 4 + dz) * CAP, CAP), :].astype(F32)
+        pown[pl.ds((arr * 4 + dz) * HALF, CAP), CA:] = (a + b).astype(BF)
+
+    def give_part(dz, arr, dx, cols, sem):
+        src = pown.at[pl.ds((arr * 4 + dz) * HALF + dx * CAP, CAP), cols]
+        dst = ret.at[pl.ds((arr * 2 + dx) * SLOTS + dz * CAP, CAP), cols]
+        if dz == 0:
+            copy = pltpu.make_async_copy(src, dst, loc_sem.at[2 + arr * 3 + sem])
+            copy.start()
+        else:
+            copy = send(src, dst, at_z(dz))
+            late.append(copy)
+        return copy
+
     def give_back(dz, arr):
-        got = []
-        for dx in (0, 1):
-            src = pown.at[pl.ds((arr * 4 + dz) * HALF + dx * CAP, CAP)]
-            dst = ret.at[pl.ds((arr * 2 + dx) * SLOTS + dz * CAP, CAP)]
-            if dz == 0:
-                copy = pltpu.make_async_copy(src, dst, loc_sem.at[2 + arr * 2 + dx])
-                copy.start()
-            else:
-                copy = send(src, dst, at_z(dz))
-                late.append(copy)
-            got.append(copy)
-        return got
-
-    order = (1, 3, 2, 0)
-    hand = {}
-    back = {}
+        back[arr, dz] = [give_part(dz, arr, dx, A, dx) for dx in (0, 1)]
+
+    def give_last(dz, arr):
+        add_swapped(dz, arr)
+        back[arr, dz].append(give_part(dz, arr, 0, B, 2))
+
+    order = (0, 1, 3, 2)
+    hand, hand_b = {}, {}
+    back, swapped = {}, {}
     for dz in order:
         product(hid, wd, dz, 0)
         hand[dz] = hand_over(dz)
+    cot_two(1)
+    cot_two(3)
     for dz in order:
         add_up(dz, 0, hand[dz])
+        swap(dz, 0)
         pl.semaphore_signal(credit.at[dz], inc=1, device_id=to_core, device_id_type=MESH)
-        back[0, dz] = give_back(dz, 0)
-
-    for dz in (1, 3, 2):
-        z_cot1[dz].wait_recv()
-        core_cot[dz, 1] = cross(cots, dz, 1)
 
     def backward_one(dz):
+        core_wait(core_cot, dz)
         here = pl.ds(dz * SLOTS, SLOTS)
         pre[:, :FF] = dot(cots[here, :], wd[...], NN)
 
@@ -338,40 +390,29 @@
 
         loop(SLOTS // 16, act)
 
-    hand_b = {}
-    for dz in order:
-        core_wait(core_cot, dz)
-        backward_one(dz)
+    def backward_two(dz):
         hand[dz].wait_send()
         pl.semaphore_wait(credit.at[dz], 1)
         product(dgu, wgu, dz, 1)
         hand_b[dz] = hand_over(dz)
-    for dz in order:
-        add_up(dz, 1, hand_b[dz])
-        back[1, dz] = give_back(dz, 1)
-
-    for copy in late:
+
+    for dz in (0, 1, 3):
+        backward_one(dz)
+        backward_two(dz)
+    cot_two(2)
+    for dz in (1, 3, 2, 0):
+        give_back(dz, 0)
+    backward_one(2)
+
+    for copy in w_sent:
         copy.wait_send()
-    done = len(late)
-
-    def weight_grad(xh_, pair):
-        cols = pl.ds(pl.multiple_of((xh_ * 2 + pair) * 2 * SH, 128), 2 * SH)
-        where = pl.ds(pl.multiple_of((xh_ * 2 + pair) * 2 * SH, 128), 2 * SH)
-        wgu[where, :] = dot(rows[:, cols], dgu[...], TN).astype(BF)
-        wd[where, :] = dot(cots[:, cols], hid[...], TN).astype(BF)
 
     near = y // 2
-    loop(2, lambda i: weight_grad(i, 1 - near))
-    first = []
-    for xh_ in (0, 1):
-        for buf, land in ((wgu, y1gu), (wd, y1d)):
-            part = shard(buf, xh_, y_far, 0, SH // 2)
-            up = send(part, land.at[xh_], to_yup)
-            part = shard(buf, xh_, y_far, SH // 2, SH // 2)
-            dn = send(part, land.at[2 + xh_], to_ydn)
-            late += [up, dn]
-            first.append((xh_, buf, land, up, dn))
-    loop(2, lambda i: weight_grad(i, near))
+    other = 1 - xh
+
+    def weight_grad(left, right, buf, xh_, pair):
+        at = pl.ds(pl.multiple_of((xh_ * 2 + pair) * 2 * SH, 128), 2 * SH)
+        buf[at, :] = dot(left[:, at], right[...], TN).astype(BF)
 
     def add_into(buf, start, land, k):
         def tile(n):
@@ -382,23 +423,96 @@
 
         loop(SH // 2 // 16, tile)
 
-    second = []
-    for xh_, buf, land, up, dn in first:
-        land2 = y2gu if buf is wgu else y2d
+    def ring_first(buf, land, k, xh_):
+        up = send(shard(buf, xh_, y_far, 0, SH // 2), land.at[k], to_yup)
+        dn = send(shard(buf, xh_, y_far, SH // 2, SH // 2), land.at[2 + k], to_ydn)
+        late.extend([up, dn])
+        return up, dn
+
+    def ring_second(buf, land, land2, k, xh_, pair):
+        up, dn = pair
         up.wait_recv()
-        add_into(buf, (xh_ * 4 + y_up) * SH, land, xh_)
-        on_up = send(shard(buf, xh_, y_up), land2.at[xh_], to_yup)
+        add_into(buf, (xh_ * 4 + y_up) * SH, land, k)
+        on_up = send(shard(buf, xh_, y_up), land2.at[k], to_yup)
         dn.wait_recv()
-        add_into(buf, (xh_ * 4 + y_dn) * SH + SH // 2, land, 2 + xh_)
-        on_dn = send(shard(buf, xh_, y_dn), land2.at[2 + xh_], to_ydn)
-        late += [on_up, on_dn]
-        second += [on_up, on_dn]
+        add_into(buf, (xh_ * 4 + y_dn) * SH + SH // 2, land, 2 + k)
+        on_dn = send(shard(buf, xh_, y_dn), land2.at[2 + k], to_ydn)
+        late.extend([on_up, on_dn])
+        return on_up, on_dn
+
+    def owner_value(buf, land, k, xh_):
+        start = (xh_ * 4 + y) * SH
+
+        def value(r):
+            at = pl.ds(pl.multiple_of(start + r, 16), 16)
+            here = pl.ds(r, 16)
+            total = buf[at, :].astype(F32) + land[k, here, :].astype(F32)
+            return total + land[2 + k, here, :].astype(F32)
+
+        return start, value
+
+    def ring_third(buf, land, recv, pair):
+        for copy in pair:
+            copy.wait_recv()
+        start, value = owner_value(buf, land, 0, other)
+
+        def tile(n):
+            r = pl.multiple_of(n * 16, 16)
+            buf[pl.ds(pl.multiple_of(start + r, 16), 16), :] = value(r).astype(BF)
+
+        loop(SH // 16, tile)
+        copy = send(shard(buf, other, y), recv, to_xh)
+        late.append(copy)
+        return copy
+
+    def ring_last(buf, land, recv, out, pair, copy):
+        for c_ in pair:
+            c_.wait_recv()
+        copy.wait_recv()
+        _, value = owner_value(buf, land, 1, xh)
+
+        def tile(n):
+            r = pl.multiple_of(n * 16, 16)
+            out[pl.ds(r, 16), :] = value(r) + recv[pl.ds(r, 16), :].astype(F32)
+
+        loop(SH // 16, tile)
+
+    weight_grad(cots, hid, wd, other, 1 - near)
+    d_a = ring_first(wd, y1d, 0, other)
+    weight_grad(cots, hid, wd, xh, 1 - near)
+    d_b = ring_first(wd, y1d, 1, xh)
+    weight_grad(cots, hid, wd, other, near)
+    weight_grad(cots, hid, wd, xh, near)
+    backward_two(2)
+    for dz in (1, 3, 0):
+        add_up(dz, 1, hand_b[dz])
+        swap(dz, 1)
+    for dz in (1, 3, 2, 0):
+        give_last(dz, 0)
+    weight_grad(rows, dgu, wgu, other, 1 - near)
+    gu_a = ring_first(wgu, y1gu, 0, other)
+    d_a = ring_second(wd, y1d, y2d, 0, other, d_a)
+    weight_grad(rows, dgu, wgu, xh, 1 - near)
+    gu_b = ring_first(wgu, y1gu, 1, xh)
+    d_b = ring_second(wd, y1d, y2d, 1, xh, d_b)
+    weight_grad(rows, dgu, wgu, other, near)
+    gu_a = ring_second(wgu, y1gu, y2gu, 0, other, gu_a)
+    weight_grad(rows, dgu, wgu, xh, near)
+    gu_b = ring_second(wgu, y1gu, y2gu, 1, xh, gu_b)
+    add_up(2, 1, hand_b[2])
+    swap(2, 1)
+    for dz in (1, 3, 2, 0):
+        give_back(dz, 1)
+    d_x = ring_third(wd, y2d, xd, d_a)
+    for dz in (1, 3, 2, 0):
+        give_last(dz, 1)
+    gu_x = ring_third(wgu, y2gu, xgu, gu_a)
 
     def combine(arr):
         for copy in back[arr, 0]:
             copy.wait()
         for dz in (1, 3, 2):
-            for copy in back[arr, dz]:
+            for copy in back[arr, dz][:2]:
                 copy.wait_recv()
 
         def pick(mat):
@@ -409,80 +523,45 @@
         mat_p = pick(gates_p[...])
 
         def tile(n):
-            cols = pl.ds(pl.multiple_of(n * 512, 512), 512)
+            cols = pl.ds(pl.multiple_of(n * 896, 128), 896)
             part = ret[pl.ds((arr * 2 + 1) * SLOTS, SLOTS), cols]
             fin_send[arr, :, cols] = dot(mat_p, part, TN).astype(BF)
 
-        loop(D // 512, tile)
+        loop(CA // 896, tile)
         copy = send(fin_send.at[arr], fin_recv.at[arr], to_x)
         late.append(copy)
         return copy, pick(gates[...])
 
     def finish(arr, copy, mat, dst):
+        for dz in (1, 3, 2):
+            back[arr, dz][2].wait_recv()
+        part = ret[pl.ds(arr * 2 * SLOTS, SLOTS), CA:]
+        dst[:, CA:] = dot(mat, part, TN).astype(BF)
         copy.wait_recv()
 
         def tile(n):
-            cols = pl.ds(pl.multiple_of(n * 512, 512), 512)
+            cols = pl.ds(pl.multiple_of(n * 896, 128), 896)
             part = ret[pl.ds(arr * 2 * SLOTS, SLOTS), cols]
             total = dot(mat, part, TN) + fin_recv[arr, :, cols].astype(F32)
             dst[:, cols] = total.astype(BF)
 
-        loop(D // 512, tile)
+        loop(CA // 896, tile)
 
     comb0 = combine(0)
-
-    for copy in second:
-        copy.wait_recv()
-
-    def owner_sum(xh_, buf, land):
-        start = (xh_ * 4 + y) * SH
-
-        def value(r):
-            at = pl.ds(pl.multiple_of(start + r, 16), 16)
-            here = pl.ds(r, 16)
-            total = buf[at, :].astype(F32) + land[xh_, here, :].astype(F32)
-            return total + land[2 + xh_, here, :].astype(F32)
-
-        return start, value
-
-    last = []
-    for buf, land, out, recv in ((wgu, y2gu, ggu_ref, xgu), (wd, y2d, gd_ref, xd)):
-        start, value = owner_sum(1 - xh, buf, land)
-
-        def tile(n, buf=buf, start=start, value=value):
-            r = pl.multiple_of(n * 16, 16)
-            buf[pl.ds(pl.multiple_of(start + r, 16), 16), :] = value(r).astype(BF)
-
-        loop(SH // 16, tile)
-        copy = send(shard(buf, 1 - xh, y), recv, to_xh)
-        late.append(copy)
-        last.append(copy)
+    ring_last(wd, y2d, xd, gd_ref, d_b, d_x)
     finish(0, *comb0, out_ref)
     comb1 = combine(1)
-    for copy, (buf, land, out, recv) in zip(
-        last, ((wgu, y2gu, ggu_ref, xgu), (wd, y2d, gd_ref, xd))
-    ):
-        copy.wait_recv()
-        start, value = owner_sum(xh, buf, land)
-
-        def tile(n, out=out, value=value, recv=recv):
-            r = pl.multiple_of(n * 16, 16)
-            out[pl.ds(r, 16), :] = value(r) + recv[pl.ds(r, 16), :].astype(F32)
-
-        loop(SH // 16, tile)
+    ring_last(wgu, y2gu, xgu, ggu_ref, gu_b, gu_x)
     finish(1, *comb1, tgrad_ref)
 
-    for copy in late[done:]:
+    for copy in late:
         copy.wait_send()
-    for copies in (z_cot0, z_cot1):
-        for copy in copies.values():
-            copy.wait_send()
     for dz in order:
         hand_b[dz].wait_send()
     assert used[0] <= N_COPY, used[0]
 
 
-N_COPY = 128
+N_COPY = 160
 
 
 def exchange(gates, tok, cot, wgu, wd):
@@ -495,9 +574,9 @@
     ]
     scratch = [
         pltpu.VMEM((SLOTS, TOK), BF),
-        pltpu.VMEM((TOK, D), BF),
-        pltpu.VMEM((TOK, D), BF),
-        pltpu.VMEM((6 * CAP, D), BF),
+        pltpu.VMEM((TOK, CA), BF),
+        pltpu.VMEM((TOK, CA), BF),
+        pltpu.VMEM((12 * CAP, D), BF),
         pltpu.VMEM((ROWS, D), BF),
         pltpu.VMEM((ROWS, D), BF),
         pltpu.VMEM((D, 2 * FF), BF),
@@ -509,8 +588,9 @@
         pltpu.VMEM((8 * HALF, D), BF),
         pltpu.VMEM((4 * HALF, D), BF),
         pltpu.VMEM((4 * SLOTS, D), BF),
-        pltpu.VMEM((2, TOK, D), BF),
-        pltpu.VMEM((2, TOK, D), BF),
+        pltpu.VMEM((2, TOK, CA), BF),
+        pltpu.VMEM((2, TOK, CA), BF),
+        pltpu.VMEM((2 * SLOTS, CB), BF),
         pltpu.VMEM((4, SH // 2, 2 * FF), BF),
         pltpu.VMEM((4, SH // 2, FF), BF),
         pltpu.VMEM((4, SH, 2 * FF), BF),
@@ -519,7 +599,7 @@
         pltpu.VMEM((SH, FF), BF),
         pltpu.SemaphoreType.DMA((N_COPY,)),
         pltpu.SemaphoreType.DMA((N_COPY,)),
-        pltpu.SemaphoreType.DMA((6,)),
+        pltpu.SemaphoreType.DMA((8,)),
         pltpu.SemaphoreType.REGULAR((4,)),
     ]
     return pl.pallas_call(

time: 257 us -> 191 us (0.74)
  Pallas kernels: 240 us -> 173 us
    pallas_call x1, Pallas kernels: 240 us -> 173 us  [exchange(): pl.pallas_call(kernel, out_shape=shapes, in_specs=[vmem] * 5, out_specs=[...]
where the time goes in v2:
time: 191 us; the launch traced here: 190 us
  Pallas kernels  173 us (91%)
  other arithmetic  10.5 us (5%)
  local copies, waits for them, and re-layouts  5.56 us (3%)
    pallas_call x1, Pallas kernels, exchange(): pl.pallas_call(kernel, out_shape=shapes, in_specs=[vmem] * 5, out_specs=[...  173 us
    sub x1, other arithmetic, per_device(): updated = masters - learn_rate * adam_step  4.56 us

profile of v2, /device:TPU:32, one launch (start us, length us, event | category | flops | bytes accessed | tf_op | source)
XLA Modules:
  0.0 190.1 jit_solution(9292079157919963520)
XLA Ops:
  0.6 0.0 copy-start
  0.7 0.9 compare_reduce_fusion
  1.5 0.1 eq.41
  1.6 0.7 convert_element_type.18
  2.3 0.8 fusion.3
  3.1 0.1 copy.18
  3.2 0.2 reduce_window_sum.11
  3.4 0.1 copy.19
  3.4 0.8 fusion.1.gates
  4.2 1.8 convert_bitcast_fusion.wd_in
  6.0 0.0 copy-done
  6.0 0.1 convert.8
  6.0 0.1 slice_bitcast_fusion.4
  6.1 0.8 pad_maximum_fusion.2.wgu_in
  6.9 173.3 %experts.1 = (bf16[128,2560]{1,0:T(8,128)(2,1)}, bf16[128,2560]{1,0:T(8,128)(2,1)}, f32[320,768]{1,0:T(8,128)}, f32[320,384]{1,0:T(8,128)}) custom-call(bf16[320,128]{1,0:T(8,128)(2,1)} %fusion.1.gates, bf16[128,2560]{1,0:T(8,128)(2,1)} %tok.1, bf16[128,2560]{1,0:T(8,128)(2,1)} %cot.1, bf16[320,768]{1,0:T(8,128)(2,1)} %pad_maximum_fusion.2.wgu_in, ...), custom_call_target="tpu_custom_call" | custom-call | flops 22649241600 | bytes 4194304 | tf_op jit(solution)/shard_map/experts/pallas_call | solution.py:605
  180.2 0.0 copy-start.1
  180.3 0.0 copy-start.2
  180.3 0.0 copy-start.5
  180.3 1.4 slice_bitcast_fusion.2
  181.7 0.1 copy-done.1
  181.7 0.1 copy-done.2
  181.9 0.1 copy-done.5
  182.0 4.6 %multiply_subtract_fusion = (f32[3,1,320,384]{3,2,1,0:T(8,128)S(1)}, f32[3,1,320,384]{3,2,1,0:T(8,128)}, f32[3,1,320,384]{3,2,1,0:T(8,128)}) fusion(f32[1,1,320,384]{3,2,1,0:T(8,128)S(1)} %bitcast.30, f32[2,1,320,384]{3,2,1,0:T(8,128)S(1)} %copy-done.1, f32[1,1,320,384]{3,2,1,0:T(8,128)S(1)} %bitcast.31, f32[1,1,320,384]{3,2,1,0:T(8,128)S(1)} %get-tuple-element.18, ...), kind=kLoop, calls=%fused_computation.4 | loop fusion | flops 6635520 | bytes 10321920 | tf_op jit(solution)/shard_map/sub | solution.py:647
  186.6 0.0 copy-start.4
  186.6 0.8 slice_bitcast_fusion
  187.4 0.0 copy-start.3
  187.4 1.0 slice.28
  188.4 0.0 copy-done.4
  188.4 0.8 copy.22
  189.2 0.0 copy-done.3
  189.2 0.8 copy.23
  (4 shorter events, 0.0 us)
Async XLA Ops:
  0.6 5.3 %copy-start = (f32[2,1,320,384]{3,2,1,0:T(8,128)S(1)}, f32[2,1,320,384]{3,2,1,0:T(8,128)}, u32[]{:S(2)}) copy-start(f32[2,1,320,384]{3,2,1,0:T(8,128)} %param.12) | copy-start | bytes 2949124
  180.2 1.5 copy-start.1
  180.3 1.6 copy-start.2
  180.3 1.7 copy-start.5
  186.6 1.8 copy-start.4
  187.4 1.9 copy-start.3

commit v3 on v2

v3 whole, which is shorter than its diff:
```python
import functools

import jax
import jax.numpy as jnp
from jax import lax
from jax.experimental import pallas as pl
from jax.experimental.pallas import tpu as pltpu
from jax.sharding import PartitionSpec as P

MESH = pl.DeviceIdType.MESH
BF = jnp.bfloat16
F32 = jnp.float32
CAP = 80
WIN = 4
TOK = 128
D = 2560
FF = 384
SH = 320
SLOTS = WIN * CAP
ROWS = 16 * CAP
HALF = 2 * CAP
CA = 1792
CB = D - CA
A, B = pl.ds(0, CA), pl.ds(CA, CB)

beta_one = 0.9
beta_two = 0.95
learn_rate = 0.0003
decay_rate = 0.1
adam_eps = 1e-08
bias_one = 1.0 - 0.9**10
bias_two = 1.0 - 0.95**10

NN = (((1,), (0,)), ((), ()))
NT = (((1,), (1,)), ((), ()))
TN = (((0,), (0,)), ((), ()))


def dot(a, b, dims):
    return lax.dot_general(a, b, dims, preferred_element_type=F32)


def loop(count, body):
    lax.fori_loop(0, count, lambda i, c: (body(i), c)[1], 0)


def slot_gates(z, ids_ref, gate_ref, gates):
    ids = ids_ref[...]
    value = gate_ref[...].astype(F32)
    down = lax.broadcasted_iota(jnp.int32, (TOK, TOK), 0)
    lane = lax.broadcasted_iota(jnp.int32, (TOK, TOK), 1)
    row = lax.broadcasted_iota(jnp.int32, (8, TOK), 0)
    named = jnp.zeros((8, TOK), F32)
    match, weight = [], []
    for dz in range(WIN):
        hit = ids == (z - dz + WIN) % WIN
        match.append(jnp.sum(jnp.where(hit, 1.0, 0.0), axis=0, keepdims=True))
        weight.append(jnp.sum(jnp.where(hit, value, 0.0), axis=0, keepdims=True))
        named = jnp.where(row == dz, match[dz], named)
    upto = jnp.where(down <= lane, 1.0, 0.0).astype(BF)
    count = dot(named.astype(BF), upto, NN).astype(jnp.int32)
    slot = lax.broadcasted_iota(jnp.int32, (CAP, TOK), 0)
    for dz in range(WIN):
        place = jnp.where(match[dz] > 0, count[dz : dz + 1] - 1, -1)
        gates[pl.ds(dz * CAP, CAP), :] = jnp.where(slot == place, weight[dz], 0.0).astype(BF)


def kernel(
    ids_ref,
    gate_ref,
    tok_hbm,
    cot_hbm,
    proj_in,
    proj_out,
    out_ref,
    tgrad_ref,
    ggu_ref,
    gd_ref,
    gates,
    gates_p,
    tok_p,
    cot_p,
    slots,
    slots_p,
    rows,
    cots,
    wgu,
    wd,
    hid,
    dgu,
    psend,
    pown,
    precv,
    ret,
    fin_recv,
    xret,
    ggu,
    gd,
    y1gu,
    y1d,
    y2gu,
    y2d,
    xgu,
    xd,
    send_sem,
    recv_sem,
    loc_sem,
    credit,
):
    tok, cot, pre = out_ref, tgrad_ref, ggu_ref
    g = lax.axis_index("group")
    m = lax.axis_index("member")
    xh, y = g // 4, g % 4
    z, xc = m // 4, m % 4
    x, c = xc // 2, xc % 2
    to_core = (g, z * 4 + x * 2 + (1 - c))
    to_x = (g, z * 4 + (1 - x) * 2 + c)

    def at_z(step):
        return (g, ((z + step) % 4) * 4 + xc)

    y_up, y_dn, y_far = (y + 1) % 4, (y + 3) % 4, (y + 2) % 4
    to_yup = (xh * 4 + y_up, m)
    to_ydn = (xh * 4 + y_dn, m)
    to_xh = ((1 - xh) * 4 + y, m)

    used = [0]

    def send(src, dst, target):
        i = used[0]
        used[0] += 1
        copy = pltpu.make_async_remote_copy(
            src_ref=src,
            dst_ref=dst,
            send_sem=send_sem.at[i],
            recv_sem=recv_sem.at[i],
            device_id=target,
            device_id_type=MESH,
        )
        copy.start()
        return copy

    loads = [
        pltpu.make_async_copy(tok_hbm, tok, loc_sem.at[8]),
        pltpu.make_async_copy(proj_in.at[0, 0], pre.at[:, pl.ds(0, FF)], loc_sem.at[9]),
        pltpu.make_async_copy(proj_in.at[1, 0], pre.at[:, pl.ds(FF, FF)], loc_sem.at[10]),
        pltpu.make_async_copy(proj_out.at[0], gd_ref, loc_sem.at[11]),
        pltpu.make_async_copy(cot_hbm, cot, loc_sem.at[12]),
    ]
    for copy in loads:
        copy.start()
    barrier = pltpu.get_barrier_semaphore()
    for other in (to_core, to_x, at_z(1), at_z(2), at_z(3), to_yup, to_ydn, to_xh):
        pl.semaphore_signal(barrier, inc=1, device_id=other, device_id_type=MESH)
    slot_gates(z, ids_ref, gate_ref, gates)
    for copy in loads[:4]:
        copy.wait()
    own = pl.ds(pl.multiple_of((xh * 4 + y) * SH, SH), SH)
    wgu[own, :] = pre[...].astype(BF)
    wd[own, :] = gd_ref[...].astype(BF)
    pl.semaphore_wait(barrier, 8)

    def shard(ref, xh_, y_, first=0, count=SH):
        start = pl.multiple_of((xh_ * 4 + y_) * SH + first, 16)
        return ref.at[pl.ds(start, count)]

    def block(ref, dz, dc, dx):
        return ref.at[pl.ds(dz * SLOTS + dc * HALF + dx * CAP, CAP)]

    late = []

    c_gates = send(gates, gates_p, to_x)
    late.append(c_gates)

    def w_first(buf):
        part = shard(buf, xh, y)
        up = send(part, part, to_yup)
        dn = send(part, part, to_ydn)
        late.extend([up, dn])
        return up, dn

    def w_far(buf):
        far = send(shard(buf, xh, y), shard(buf, xh, y), to_xh)
        late.append(far)
        return far

    def w_second(buf, far):
        far.wait_recv()
        part = shard(buf, 1 - xh, y)
        up = send(part, part, to_yup)
        dn = send(part, part, to_ydn)
        late.extend([up, dn])
        return up, dn

    def w_forward(buf, xh_, pair):
        up, dn = pair
        up.wait_recv()
        part = shard(buf, xh_, y_dn, 0, SH // 2)
        on_up = send(part, part, to_yup)
        dn.wait_recv()
        part = shard(buf, xh_, y_up, SH // 2, SH // 2)
        on_dn = send(part, part, to_ydn)
        late.extend([on_up, on_dn])
        return on_up, on_dn

    gu0 = w_first(wgu)
    gu_far = w_far(wgu)

    def fill(mat_ref, val_ref, dst, dx, base, gated, width, step):
        held = (slots, slots_p)[dx]
        mat = mat_ref[...]
        if not gated:
            mat = jnp.where(mat > 0, jnp.ones_like(mat), jnp.zeros_like(mat))

        def tile(n):
            cols = pl.ds(pl.multiple_of(n * step, 128), step)
            val = dot(mat, val_ref[:, cols], NN).astype(BF)
            dst[pl.ds(dx * CAP, CAP), cols] = val[:CAP]
            held[pl.ds(base * 3 * CAP, 3 * CAP), cols] = val[CAP:]

        loop(width // step, tile)

    def spread(dst, dx, base, dz):
        src = (slots, slots_p)[dx].at[pl.ds((base * 3 + dz - 1) * CAP, CAP)]
        land = block(dst, dz, 0, dx)
        if dx == 1:
            land = land.at[:, A]
        copy = send(src, land, at_z(4 - dz))
        late.append(copy)
        return copy

    def cross(dst, dz, dx, cols):
        copy = send(
            block(dst, dz, 0, dx).at[:, cols], block(dst, dz, 1, dx).at[:, cols], to_core
        )
        late.append(copy)
        return copy

    def own_in(dst, table, dz):
        table[dz, 0] = cross(dst, dz, 0, pl.ds(0, D))

    def own_on(dst, table, dz):
        copy = send(block(dst, dz, 0, 0).at[:, B], block(dst, dz, 0, 1).at[:, B], to_x)
        late.append(copy)
        table[dz, "x"] = copy

    def last_in(dst, table, dz):
        table[dz, "x"].wait_recv()
        table[dz, 2] = cross(dst, dz, 1, B)

    core_tok, core_cot = {}, {}
    fill(gates, tok, rows, 0, 0, False, D, 512)
    z_tok0 = {dz: spread(rows, 0, 0, dz) for dz in (1, 3, 2)}
    own_in(rows, core_tok, 0)
    c_tok = send(tok.at[:, A], tok_p, to_x)
    loads[4].wait()
    fill(gates, cot, cots, 0, 1, True, D, 512)
    gu2 = w_forward(wgu, xh, gu0)
    gu1 = w_second(wgu, gu_far)
    for dz in (1, 3, 2):
        z_tok0[dz].wait_recv()
        own_in(rows, core_tok, dz)
    z_cot0 = {2: spread(cots, 0, 1, 2)}
    c_gates.wait_recv()
    c_tok.wait_recv()
    for dz in (0, 1, 3, 2):
        own_on(rows, core_tok, dz)
    fill(gates_p, tok_p, rows, 1, 0, False, CA, 896)
    z_tok1 = {dz: spread(rows, 1, 0, dz) for dz in (1, 3, 2)}
    core_tok[0, 1] = cross(rows, 0, 1, A)
    d0 = w_first(wd)
    d_far = w_far(wd)
    gu3 = w_forward(wgu, 1 - xh, gu1)
    c_cot = send(cot.at[:, A], cot_p, to_x)
    z_cot0[1] = spread(cots, 0, 1, 1)
    z_cot0[3] = spread(cots, 0, 1, 3)
    d2 = w_forward(wd, xh, d0)
    d1 = w_second(wd, d_far)
    last_in(rows, core_tok, 0)
    own_in(cots, core_cot, 0)
    own_on(cots, core_cot, 0)
    for dz in (1, 3, 2):
        z_tok1[dz].wait_recv()
        core_tok[dz, 1] = cross(rows, dz, 1, A)
    for dz in (1, 3, 2):
        last_in(rows, core_tok, dz)

    for copy in gu2 + gu3:
        copy.wait_recv()

    def forward_one(dz):
        here = pl.ds(dz * SLOTS, SLOTS)

        pre[...] = dot(rows[here, :], wgu[...], NN)

        def act(n):
            src = pl.ds(pl.multiple_of(n * 16, 16), 16)
            dst = pl.ds(pl.multiple_of(dz * SLOTS + n * 16, 16), 16)
            gate, up = pre[src, :FF], pre[src, FF:]
            sig = jax.nn.sigmoid(gate)
            active = gate * sig
            hid[dst, :] = (active * up).astype(BF)
            dgu[dst, :FF] = (up * (sig * (1.0 + gate * (1.0 - sig)))).astype(BF)
            dgu[dst, FF:] = active.astype(BF)

        loop(SLOTS // 16, act)

    def core_wait(table, dz):
        for part in range(3):
            table[dz, part].wait_recv()

    def cot_one(dz):
        z_cot0[dz].wait_recv()
        own_in(cots, core_cot, dz)
        own_on(cots, core_cot, dz)

    def cot_two(dz):
        z_cot1[dz].wait_recv()
        core_cot[dz, 1] = cross(cots, dz, 1, A)
        last_in(cots, core_cot, dz)

    core_wait(core_tok, 0)
    forward_one(0)
    core_wait(core_tok, 1)
    forward_one(1)
    c_cot.wait_recv()
    fill(gates_p, cot_p, cots, 1, 1, True, CA, 896)
    z_cot1 = {dz: spread(cots, 1, 1, dz) for dz in (1, 3, 2)}
    core_cot[0, 1] = cross(cots, 0, 1, A)
    d3 = w_forward(wd, 1 - xh, d1)
    last_in(cots, core_cot, 0)
    core_wait(core_tok, 3)
    forward_one(3)
    core_wait(core_tok, 2)
    forward_one(2)
    for dz in (1, 3, 2):
        cot_one(dz)

    for copy in d2 + d3:
        copy.wait_recv()

    def product(left, right, dz, arr):
        here = pl.ds(dz * SLOTS, SLOTS)

        def tile(n):
            cols = pl.ds(pl.multiple_of(n * 1280, 256), 1280)
            val = dot(left[here, :], right[cols, :], NT).astype(BF)
            pown[pl.ds((arr * 4 + dz) * HALF, HALF), cols] = val[:HALF]
            psend[pl.ds(dz * HALF, HALF), cols] = val[HALF:]

        loop(D // 1280, tile)

    def hand_over(dz):
        part = pl.ds(dz * HALF, HALF)
        return send(psend.at[part], precv.at[part], to_core)

    def add_up(dz, arr, copy):
        copy.wait_recv()

        def tile(n):
            k = pl.multiple_of(n * 16, 16)
            a = pown[pl.ds((arr * 4 + dz) * HALF + k, 16), :].astype(F32)
            b = precv[pl.ds(dz * HALF + k, 16), :].astype(F32)
            pown[pl.ds((arr * 4 + dz) * HALF + k, 16), :] = (a + b).astype(BF)

        loop(HALF // 16, tile)

    def swap(dz, arr):
        src = pown.at[pl.ds((arr * 4 + dz) * HALF + CAP, CAP), B]
        copy = send(src, xret.at[pl.ds((arr * 4 + dz) * CAP, CAP)], to_x)
        late.append(copy)
        swapped[arr, dz] = copy

    def add_swapped(dz, arr):
        swapped[arr, dz].wait_recv()
        a = pown[pl.ds((arr * 4 + dz) * HALF, CAP), CA:].astype(F32)
        b = xret[pl.ds((arr * 4 + dz) * CAP, CAP), :].astype(F32)
        pown[pl.ds((arr * 4 + dz) * HALF, CAP), CA:] = (a + b).astype(BF)

    parts = (pl.ds(0, CA // 2), pl.ds(CA // 2, CA // 2), B)

    def give(dz, arr, n, dx):
        src = pown.at[pl.ds((arr * 4 + dz) * HALF + dx * CAP, CAP), parts[n]]
        dst = ret.at[pl.ds((arr * 2 + dx) * SLOTS + dz * CAP, CAP), parts[n]]
        if dz == 0:
            copy = pltpu.make_async_copy(src, dst, loc_sem.at[13 + arr * 5 + n * 2 + dx])
            copy.start()
        else:
            copy = send(src, dst, at_z(dz))
            late.append(copy)
        back[arr, n, dz, dx] = copy

    def give_back(arr, n):
        for dz in (1, 3, 2, 0):
            give(dz, arr, n, 0)
            give(dz, arr, n, 1)

    def give_last(arr):
        for dz in (1, 3, 2, 0):
            add_swapped(dz, arr)
            give(dz, arr, 2, 0)

    def given(arr, n):
        for dx in (0, 1) if n < 2 else (0,):
            back[arr, n, 0, dx].wait()
            for dz in (1, 3, 2):
                back[arr, n, dz, dx].wait_recv()

    order = (0, 1, 3, 2)
    hand, hand_b = {}, {}
    back, swapped = {}, {}
    for dz in order:
        product(hid, wd, dz, 0)
        hand[dz] = hand_over(dz)
    for dz in order:
        add_up(dz, 0, hand[dz])
        swap(dz, 0)
        pl.semaphore_signal(credit.at[dz], inc=1, device_id=to_core, device_id_type=MESH)

    def backward_one(dz):
        here = pl.ds(dz * SLOTS, SLOTS)
        pre[:, :FF] = dot(cots[here, :], wd[...], NN)

        def act(n):
            src = pl.ds(pl.multiple_of(n * 16, 16), 16)
            dst = pl.ds(pl.multiple_of(dz * SLOTS + n * 16, 16), 16)
            dh = pre[src, :FF]
            dgu[dst, :FF] = (dgu[dst, :FF].astype(F32) * dh).astype(BF)
            dgu[dst, FF:] = (dgu[dst, FF:].astype(F32) * dh).astype(BF)

        loop(SLOTS // 16, act)

    def backward_two(dz):
        hand[dz].wait_send()
        pl.semaphore_wait(credit.at[dz], 1)
        product(dgu, wgu, dz, 1)
        hand_b[dz] = hand_over(dz)

    give_back(0, 0)
    give_back(0, 1)
    for dz in (1, 3, 2):
        cot_two(dz)
    core_wait(core_cot, 0)
    backward_one(0)
    backward_two(0)
    for dz in (1, 3, 2):
        core_wait(core_cot, dz)

    near = y // 2
    other = 1 - xh

    def weight_grad(left, right, buf, xh_, pair):
        at = pl.ds(pl.multiple_of((xh_ * 2 + pair) * 2 * SH, 128), 2 * SH)
        buf[at, :] = dot(left[:, at], right[...], TN).astype(BF)

    def add_into(buf, start, land, k):
        def tile(n):
            r = pl.multiple_of(n * 16, 16)
            at = pl.ds(pl.multiple_of(start + r, 16), 16)
            a = buf[at, :].astype(F32) + land[k, pl.ds(r, 16), :].astype(F32)
            buf[at, :] = a.astype(BF)

        loop(SH // 2 // 16, tile)

    def ring_first(buf, land, k, xh_):
        up = send(shard(buf, xh_, y_far, 0, SH // 2), land.at[k], to_yup)
        dn = send(shard(buf, xh_, y_far, SH // 2, SH // 2), land.at[2 + k], to_ydn)
        late.extend([up, dn])
        return up, dn

    def ring_second(buf, land, land2, k, xh_, pair):
        up, dn = pair
        up.wait_recv()
        add_into(buf, (xh_ * 4 + y_up) * SH, land, k)
        on_up = send(shard(buf, xh_, y_up), land2.at[k], to_yup)
        dn.wait_recv()
        add_into(buf, (xh_ * 4 + y_dn) * SH + SH // 2, land, 2 + k)
        on_dn = send(shard(buf, xh_, y_dn), land2.at[2 + k], to_ydn)
        late.extend([on_up, on_dn])
        return on_up, on_dn

    def owner_value(buf, land, k, xh_):
        start = (xh_ * 4 + y) * SH

        def value(r):
            at = pl.ds(pl.multiple_of(start + r, 16), 16)
            here = pl.ds(r, 16)
            total = buf[at, :].astype(F32) + land[k, here, :].astype(F32)
            return total + land[2 + k, here, :].astype(F32)

        return start, value

    def ring_third(buf, land, recv, pair):
        for copy in pair:
            copy.wait_recv()
        start, value = owner_value(buf, land, 0, other)

        def tile(n):
            r = pl.multiple_of(n * 16, 16)
            buf[pl.ds(pl.multiple_of(start + r, 16), 16), :] = value(r).astype(BF)

        loop(SH // 16, tile)
        copy = send(shard(buf, other, y), recv, to_xh)
        late.append(copy)
        return copy

    def ring_last(buf, land, recv, out, pair, copy):
        for c_ in pair:
            c_.wait_recv()
        copy.wait_recv()
        _, value = owner_value(buf, land, 1, xh)

        def tile(n):
            r = pl.multiple_of(n * 16, 16)
            out[pl.ds(r, 16), :] = value(r) + recv[pl.ds(r, 16), :].astype(F32)

        loop(SH // 16, tile)

    def pick(mat_ref, arr):
        mat = mat_ref[...]
        return jnp.where(mat > 0, jnp.ones_like(mat), jnp.zeros_like(mat)) if arr else mat

    fins = {}

    def combine(arr, n):
        given(arr, n)
        held = (tok_p, cot_p)[arr]
        part = ret[pl.ds((arr * 2 + 1) * SLOTS, SLOTS), parts[n]]
        held[:, parts[n]] = dot(pick(gates_p, arr), part, TN).astype(BF)
        copy = send(held.at[:, parts[n]], fin_recv.at[arr, :, parts[n]], to_x)
        late.append(copy)
        fins[arr, n] = copy

    def finish(arr, n, dst):
        if n == 2:
            given(arr, n)
        part = ret[pl.ds(arr * 2 * SLOTS, SLOTS), parts[n]]
        total = dot(pick(gates, arr), part, TN)
        if n < 2:
            fins[arr, n].wait_recv()
            total = total + fin_recv[arr, :, parts[n]].astype(F32)
        dst[:, parts[n]] = total.astype(BF)

    def settle(dz):
        add_up(dz, 1, hand_b[dz])
        swap(dz, 1)

    weight_grad(cots, hid, gd, other, 1 - near)
    d_a = ring_first(gd, y1d, 0, other)
    weight_grad(cots, hid, gd, xh, 1 - near)
    d_b = ring_first(gd, y1d, 1, xh)
    weight_grad(cots, hid, gd, other, near)
    weight_grad(cots, hid, gd, xh, near)
    settle(0)
    backward_one(1)
    backward_two(1)
    d_a = ring_second(gd, y1d, y2d, 0, other, d_a)
    d_b = ring_second(gd, y1d, y2d, 1, xh, d_b)
    backward_one(3)
    settle(1)
    backward_two(3)
    give_last(0)
    backward_one(2)
    settle(3)
    weight_grad(rows, dgu, ggu, other, 1 - near)
    gu_a = ring_first(ggu, y1gu, 0, other)
    backward_two(2)
    weight_grad(rows, dgu, ggu, other, near)
    settle(2)
    give_back(1, 0)
    weight_grad(rows, dgu, ggu, xh, 1 - near)
    gu_b = ring_first(ggu, y1gu, 1, xh)
    gu_a = ring_second(ggu, y1gu, y2gu, 0, other, gu_a)
    d_x = ring_third(gd, y2d, xd, d_a)
    weight_grad(rows, dgu, ggu, xh, near)
    c_tok.wait_send()
    c_cot.wait_send()
    combine(0, 0)
    combine(0, 1)
    give_back(1, 1)
    give_last(1)
    finish(0, 2, out_ref)
    gu_b = ring_second(ggu, y1gu, y2gu, 1, xh, gu_b)
    ring_last(gd, y2d, xd, gd_ref, d_b, d_x)
    finish(0, 0, out_ref)
    finish(0, 1, out_ref)
    gu_x = ring_third(ggu, y2gu, xgu, gu_a)
    combine(1, 0)
    combine(1, 1)
    finish(1, 2, tgrad_ref)
    finish(1, 0, tgrad_ref)
    ring_last(ggu, y2gu, xgu, ggu_ref, gu_b, gu_x)
    finish(1, 1, tgrad_ref)

    for copy in late:
        copy.wait_send()
    for dz in order:
        hand_b[dz].wait_send()
    assert used[0] <= N_COPY, used[0]


N_COPY = 200


def exchange(ids, gates, tok, cot, proj_in, proj_out):
    vmem = pl.BlockSpec(memory_space=pltpu.VMEM)
    hbm = pl.BlockSpec(memory_space=pl.ANY)
    shapes = [
        jax.ShapeDtypeStruct((TOK, D), BF),
        jax.ShapeDtypeStruct((TOK, D), BF),
        jax.ShapeDtypeStruct((SH, 2 * FF), F32),
        jax.ShapeDtypeStruct((SH, FF), F32),
    ]
    scratch = [
        pltpu.VMEM((SLOTS, TOK), BF),
        pltpu.VMEM((SLOTS, TOK), BF),
        pltpu.VMEM((TOK, CA), BF),
        pltpu.VMEM((TOK, CA), BF),
        pltpu.VMEM((6 * CAP, D), BF),
        pltpu.VMEM((6 * CAP, CA), BF),
        pltpu.VMEM((ROWS, D), BF),
        pltpu.VMEM((ROWS, D), BF),
        pltpu.VMEM((D, 2 * FF), BF),
        pltpu.VMEM((D, FF), BF),
        pltpu.VMEM((ROWS, FF), BF),
        pltpu.VMEM((ROWS, 2 * FF), BF),
        pltpu.VMEM((4 * HALF, D), BF),
        pltpu.VMEM((8 * HALF, D), BF),
        pltpu.VMEM((4 * HALF, D), BF),
        pltpu.VMEM((4 * SLOTS, D), BF),
        pltpu.VMEM((2, TOK, CA), BF),
        pltpu.VMEM((2 * SLOTS, CB), BF),
        pltpu.VMEM((D, 2 * FF), BF),
        pltpu.VMEM((D, FF), BF),
        pltpu.VMEM((4, SH // 2, 2 * FF), BF),
        pltpu.VMEM((4, SH // 2, FF), BF),
        pltpu.VMEM((4, SH, 2 * FF), BF),
        pltpu.VMEM((4, SH, FF), BF),
        pltpu.VMEM((SH, 2 * FF), BF),
        pltpu.VMEM((SH, FF), BF),
        pltpu.SemaphoreType.DMA((N_COPY,)),
        pltpu.SemaphoreType.DMA((N_COPY,)),
        pltpu.SemaphoreType.DMA((23,)),
        pltpu.SemaphoreType.REGULAR((4,)),
    ]
    return pl.pallas_call(
        kernel,
        out_shape=shapes,
        in_specs=[vmem] * 2 + [hbm] * 4,
        out_specs=[vmem] * 4,
        scratch_shapes=scratch,
        compiler_params=pltpu.CompilerParams(
            collective_id=0, has_side_effects=True, vmem_limit_bytes=64 * 2**20
        ),
        cost_estimate=pl.CostEstimate(
            flops=18 * ROWS * D * FF, bytes_accessed=2**22, transcendentals=ROWS * FF
        ),
        name="experts",
    )(ids, gates, tok, cot, proj_in, proj_out)


def adam_kernel(ggu, gd, pin, pout, first, second, out, tgrad, *outs):
    new_in, new_out, new_first, new_second, out_copy, tgrad_copy = outs
    out_copy[...] = out[...]
    tgrad_copy[...] = tgrad[...]
    for k in range(3):
        gradient = gd[...] if k == 2 else ggu[:, k * FF : (k + 1) * FF]
        master = pout[0] if k == 2 else pin[k, 0]
        m = beta_one * first[k, 0] + (1.0 - beta_one) * gradient
        v = beta_two * second[k, 0] + (1.0 - beta_two) * gradient * gradient
        step = m / bias_one / (jnp.sqrt(v / bias_two) + adam_eps) + decay_rate * master
        updated = master - learn_rate * step
        new_first[k, 0] = m
        new_second[k, 0] = v
        if k == 2:
            new_out[0] = updated
        else:
            new_in[k, 0] = updated


def adam(ggu, gd, pin, pout, first, second, out, tgrad):
    steps = 4
    part = SH // steps

    def stacked(count):
        return pl.BlockSpec((count, 1, part, FF), lambda i: (0, 0, i, 0))

    plain = [
        pl.BlockSpec((part, 2 * FF), lambda i: (i, 0)),
        pl.BlockSpec((part, FF), lambda i: (i, 0)),
    ]
    single = pl.BlockSpec((1, part, FF), lambda i: (0, i, 0))
    token = pl.BlockSpec((TOK // steps, D), lambda i: (i, 0))
    arrays = (pin, pout, first, second, out, tgrad)
    specs = [stacked(2), single, stacked(3), stacked(3), token, token]
    return pl.pallas_call(
        adam_kernel,
        out_shape=[jax.ShapeDtypeStruct(a.shape, a.dtype) for a in arrays],
        grid=(steps,),
        in_specs=plain + specs,
        out_specs=specs,
        compiler_params=pltpu.CompilerParams(vmem_limit_bytes=64 * 2**20),
        name="adam",
    )(ggu, gd, *arrays)


def per_device(
    tokens, route_ids, route_gates, out_grad, proj_in, proj_out, first_moment, second_moment
):
    layer_out, token_grad, ggu, gd = exchange(
        route_ids.T, route_gates.T, tokens, out_grad, proj_in, proj_out
    )
    new_in, new_out, new_first, new_second, layer_out, token_grad = adam(
        ggu, gd, proj_in, proj_out, first_moment, second_moment, layer_out, token_grad
    )
    return (layer_out, token_grad, new_in, new_out, new_first, new_second)


def solution(mesh):
    rows = P(("group", "member"), None)
    return jax.shard_map(
        per_device,
        mesh=mesh,
        in_specs=(
            rows,
            rows,
            rows,
            rows,
            P(None, "member", "group", None),
            P("member", "group", None),
            P(None, "member", "group", None),
            P(None, "member", "group", None),
        ),
        out_specs=(
            rows,
            rows,
            P(None, "member", "group", None),
            P("member", "group", None),
            P(None, "member", "group", None),
            P(None, "member", "group", None),
        ),
        check_vma=False,
    )
```

time: 191 us -> 152 us (0.80)
  Pallas kernels: 173 us -> 150 us
  other arithmetic: 10.5 us -> 0 us
  local copies, waits for them, and re-layouts: 5.56 us -> 0 us
    pallas_call x1 -> x2, Pallas kernels: 173 us -> 150 us  [the longest x1 143 us: exchange(): pl.pallas_call(kernel, out_shape=shapes, in_specs=[vmem] * 2 + [hbm] * 4,...]
    sub x2 -> x0, other arithmetic: 4.57 us -> none  [the longest x1 4.56 us: per_device(): updated = masters - learn_rate * adam_step]
    convert_element_type x4 -> x0, other arithmetic: 3.21 us -> none  [the longest x1 1.75 us: per_device(): wd = proj_out[0].astype(BF)]
    unnamed x14 -> x0, local copies, waits for them, and re-layouts: 2.05 us -> none
where the time goes in v3:
time: 152 us; the launch traced here: 151 us
  Pallas kernels  150 us (99%)
    pallas_call x1, Pallas kernels, exchange(): pl.pallas_call(kernel, out_shape=shapes, in_specs=[vmem] * 2 + [hbm] * 4,...  143 us
    pallas_call x1, Pallas kernels, adam(): pl.pallas_call(adam_kernel, out_shape=[jax.ShapeDtypeStruct(a.shape, a.dt...  6.52 us

profile of v3, /device:TPU:32, one launch (start us, length us, event | category | flops | bytes accessed | tf_op | source)
XLA Modules:
  0.0 150.8 jit_solution(15012542327131012976)
XLA Ops:
  0.6 143.5 %experts.1 = (bf16[128,2560]{1,0:T(8,128)(2,1)}, bf16[128,2560]{1,0:T(8,128)(2,1)}, f32[320,768]{1,0:T(8,128)}, f32[320,384]{1,0:T(8,128)}) custom-call(s32[6,128]{1,0:T(8,128)} %bitcast.2, bf16[6,128]{1,0:T(8,128)(2,1)} %bitcast.3, bf16[128,2560]{1,0:T(8,128)(2,1)} %tok_hbm.1, bf16[128,2560]{1,0:T(8,128)(2,1)} %cot_hbm.1, f32[2,1,320,384]{3,2,1,0:T(8,128)} %pin.1, ...), custom_call_target="tpu_custom_call" | custom-call | flops 22649241600 | bytes 4194304 | tf_op jit(solution)/shard_map/experts/pallas_call | solution.py:646
  144.1 6.5 %adam.1 = (f32[2,1,320,384]{3,2,1,0:T(8,128)}, f32[1,320,384]{2,1,0:T(8,128)}, f32[3,1,320,384]{3,2,1,0:T(8,128)}, f32[3,1,320,384]{3,2,1,0:T(8,128)}, bf16[128,...) custom-call(f32[320,768]{1,0:T(8,128)} %get-tuple-element.16.ggu, f32[320,384]{1,0:T(8,128)} %get-tuple-element.17.gd, ...), custom_call_target="tpu_custom_call" | custom-call | tf_op jit(solution)/shard_map/adam/pallas_call | solution.py:696

commit v4 on v3

--- a/solution.py
+++ b/solution.py
@@ -20,8 +20,9 @@
 ROWS = 16 * CAP
 HALF = 2 * CAP
 CA = 1792
-CB = D - CA
-A, B = pl.ds(0, CA), pl.ds(CA, CB)
+CC = 1536
+CF = 1536
+CG = 1792
 
 beta_one = 0.9
 beta_two = 0.95
@@ -44,7 +45,7 @@
     lax.fori_loop(0, count, lambda i, c: (body(i), c)[1], 0)
 
 
-def slot_gates(z, ids_ref, gate_ref, gates):
+def slot_table(z, ids_ref, gate_ref, table):
     ids = ids_ref[...]
     value = gate_ref[...].astype(F32)
     down = lax.broadcasted_iota(jnp.int32, (TOK, TOK), 0)
@@ -58,11 +59,18 @@
         weight.append(jnp.sum(jnp.where(hit, value, 0.0), axis=0, keepdims=True))
         named = jnp.where(row == dz, match[dz], named)
     upto = jnp.where(down <= lane, 1.0, 0.0).astype(BF)
-    count = dot(named.astype(BF), upto, NN).astype(jnp.int32)
+    count = dot(named.astype(BF), upto, NN)
+    for dz in range(WIN):
+        table[dz : dz + 1, :] = jnp.where(match[dz] > 0, count[dz : dz + 1] - 1.0, -1.0)
+        table[WIN + dz : WIN + dz + 1, :] = weight[dz]
+
+
+def slot_gates(table, gates):
     slot = lax.broadcasted_iota(jnp.int32, (CAP, TOK), 0)
     for dz in range(WIN):
-        place = jnp.where(match[dz] > 0, count[dz : dz + 1] - 1, -1)
-        gates[pl.ds(dz * CAP, CAP), :] = jnp.where(slot == place, weight[dz], 0.0).astype(BF)
+        place = table[dz : dz + 1, :].astype(jnp.int32)
+        gate = jnp.where(slot == place, table[WIN + dz : WIN + dz + 1, :], 0.0)
+        gates[pl.ds(dz * CAP, CAP), :] = gate.astype(BF)
 
 
 def kernel(
@@ -72,10 +80,16 @@
     cot_hbm,
     proj_in,
     proj_out,
+    out_hbm,
+    tgrad_hbm,
+    ggu_hbm,
+    gd_hbm,
     out_ref,
     tgrad_ref,
     ggu_ref,
     gd_ref,
+    table,
+    table_p,
     gates,
     gates_p,
     tok_p,
@@ -92,8 +106,10 @@
     pown,
     precv,
     ret,
-    fin_recv,
-    xret,
+    fin_recv0,
+    fin_recv1,
+    xret0,
+    xret1,
     ggu,
     gd,
     y1gu,
@@ -124,20 +140,28 @@
     to_ydn = (xh * 4 + y_dn, m)
     to_xh = ((1 - xh) * 4 + y, m)
 
-    used = [0]
+    used = [0, 0]
+    free = []
+    which = {}
 
     def send(src, dst, target):
         i = used[0]
         used[0] += 1
+        if free:
+            k = free.pop()
+        else:
+            k = used[1]
+            used[1] += 1
         copy = pltpu.make_async_remote_copy(
             src_ref=src,
             dst_ref=dst,
-            send_sem=send_sem.at[i],
+            send_sem=send_sem.at[k],
             recv_sem=recv_sem.at[i],
             device_id=target,
             device_id_type=MESH,
         )
         copy.start()
+        which[id(copy)] = k
         return copy
 
     loads = [
@@ -152,7 +176,8 @@
     barrier = pltpu.get_barrier_semaphore()
     for other in (to_core, to_x, at_z(1), at_z(2), at_z(3), to_yup, to_ydn, to_xh):
         pl.semaphore_signal(barrier, inc=1, device_id=other, device_id_type=MESH)
-    slot_gates(z, ids_ref, gate_ref, gates)
+    slot_table(z, ids_ref, gate_ref, table)
+    slot_gates(table, gates)
     for copy in loads[:4]:
         copy.wait()
     own = pl.ds(pl.multiple_of((xh * 4 + y) * SH, SH), SH)
@@ -169,7 +194,7 @@
 
     late = []
 
-    c_gates = send(gates, gates_p, to_x)
+    c_gates = send(table, table_p, to_x)
     late.append(c_gates)
 
     def w_first(buf):
@@ -220,11 +245,18 @@
 
         loop(width // step, tile)
 
+    def x_first(dst):
+        return pl.ds(0, CA if dst is rows else CC)
+
+    def z_first(dst):
+        return pl.ds(CA, D - CA) if dst is rows else pl.ds(CC, D - CC)
+
     def spread(dst, dx, base, dz):
         src = (slots, slots_p)[dx].at[pl.ds((base * 3 + dz - 1) * CAP, CAP)]
         land = block(dst, dz, 0, dx)
         if dx == 1:
-            land = land.at[:, A]
+            cols = x_first(dst)
+            src, land = src.at[:, cols], land.at[:, cols]
         copy = send(src, land, at_z(4 - dz))
         late.append(copy)
         return copy
@@ -240,19 +272,20 @@
         table[dz, 0] = cross(dst, dz, 0, pl.ds(0, D))
 
     def own_on(dst, table, dz):
-        copy = send(block(dst, dz, 0, 0).at[:, B], block(dst, dz, 0, 1).at[:, B], to_x)
+        cols = z_first(dst)
+        copy = send(block(dst, dz, 0, 0).at[:, cols], block(dst, dz, 0, 1).at[:, cols], to_x)
         late.append(copy)
         table[dz, "x"] = copy
 
     def last_in(dst, table, dz):
         table[dz, "x"].wait_recv()
-        table[dz, 2] = cross(dst, dz, 1, B)
+        table[dz, 2] = cross(dst, dz, 1, z_first(dst))
 
     core_tok, core_cot = {}, {}
     fill(gates, tok, rows, 0, 0, False, D, 512)
     z_tok0 = {dz: spread(rows, 0, 0, dz) for dz in (1, 3, 2)}
     own_in(rows, core_tok, 0)
-    c_tok = send(tok.at[:, A], tok_p, to_x)
+    c_tok = send(tok.at[:, x_first(rows)], tok_p, to_x)
     loads[4].wait()
     fill(gates, cot, cots, 0, 1, True, D, 512)
     gu2 = w_forward(wgu, xh, gu0)
@@ -262,16 +295,17 @@
         own_in(rows, core_tok, dz)
     z_cot0 = {2: spread(cots, 0, 1, 2)}
     c_gates.wait_recv()
+    slot_gates(table_p, gates_p)
     c_tok.wait_recv()
     for dz in (0, 1, 3, 2):
         own_on(rows, core_tok, dz)
     fill(gates_p, tok_p, rows, 1, 0, False, CA, 896)
     z_tok1 = {dz: spread(rows, 1, 0, dz) for dz in (1, 3, 2)}
-    core_tok[0, 1] = cross(rows, 0, 1, A)
+    core_tok[0, 1] = cross(rows, 0, 1, x_first(rows))
     d0 = w_first(wd)
     d_far = w_far(wd)
     gu3 = w_forward(wgu, 1 - xh, gu1)
-    c_cot = send(cot.at[:, A], cot_p, to_x)
+    c_cot = send(cot.at[:, x_first(cots)], cot_p, to_x)
     z_cot0[1] = spread(cots, 0, 1, 1)
     z_cot0[3] = spread(cots, 0, 1, 3)
     d2 = w_forward(wd, xh, d0)
@@ -281,7 +315,7 @@
     own_on(cots, core_cot, 0)
     for dz in (1, 3, 2):
         z_tok1[dz].wait_recv()
-        core_tok[dz, 1] = cross(rows, dz, 1, A)
+        core_tok[dz, 1] = cross(rows, dz, 1, x_first(rows))
     for dz in (1, 3, 2):
         last_in(rows, core_tok, dz)
 
@@ -316,25 +350,25 @@
 
     def cot_two(dz):
         z_cot1[dz].wait_recv()
-        core_cot[dz, 1] = cross(cots, dz, 1, A)
+        core_cot[dz, 1] = cross(cots, dz, 1, x_first(cots))
         last_in(cots, core_cot, dz)
 
     core_wait(core_tok, 0)
     forward_one(0)
+    c_cot.wait_recv()
+    fill(gates_p, cot_p, cots, 1, 1, True, CC, 768)
+    z_cot1 = {dz: spread(cots, 1, 1, dz) for dz in (1, 3, 2)}
+    core_cot[0, 1] = cross(cots, 0, 1, x_first(cots))
     core_wait(core_tok, 1)
     forward_one(1)
-    c_cot.wait_recv()
-    fill(gates_p, cot_p, cots, 1, 1, True, CA, 896)
-    z_cot1 = {dz: spread(cots, 1, 1, dz) for dz in (1, 3, 2)}
-    core_cot[0, 1] = cross(cots, 0, 1, A)
     d3 = w_forward(wd, 1 - xh, d1)
     last_in(cots, core_cot, 0)
     core_wait(core_tok, 3)
     forward_one(3)
+    for dz in (1, 3, 2):
+        cot_one(dz)
     core_wait(core_tok, 2)
     forward_one(2)
-    for dz in (1, 3, 2):
-        cot_one(dz)
 
     for copy in d2 + d3:
         copy.wait_recv()
@@ -365,23 +399,27 @@
 
         loop(HALF // 16, tile)
 
+    parts = [
+        (pl.ds(0, n // 2), pl.ds(n // 2, n // 2), pl.ds(n, D - n)) for n in (CF, CG)
+    ]
+    xrets = (xret0, xret1)
+
     def swap(dz, arr):
-        src = pown.at[pl.ds((arr * 4 + dz) * HALF + CAP, CAP), B]
-        copy = send(src, xret.at[pl.ds((arr * 4 + dz) * CAP, CAP)], to_x)
+        src = pown.at[pl.ds((arr * 4 + dz) * HALF + CAP, CAP), parts[arr][2]]
+        copy = send(src, xrets[arr].at[pl.ds(dz * CAP, CAP)], to_x)
         late.append(copy)
         swapped[arr, dz] = copy
 
     def add_swapped(dz, arr):
         swapped[arr, dz].wait_recv()
-        a = pown[pl.ds((arr * 4 + dz) * HALF, CAP), CA:].astype(F32)
-        b = xret[pl.ds((arr * 4 + dz) * CAP, CAP), :].astype(F32)
-        pown[pl.ds((arr * 4 + dz) * HALF, CAP), CA:] = (a + b).astype(BF)
-
-    parts = (pl.ds(0, CA // 2), pl.ds(CA // 2, CA // 2), B)
+        cols = parts[arr][2]
+        a = pown[pl.ds((arr * 4 + dz) * HALF, CAP), cols].astype(F32)
+        b = xrets[arr][pl.ds(dz * CAP, CAP), :].astype(F32)
+        pown[pl.ds((arr * 4 + dz) * HALF, CAP), cols] = (a + b).astype(BF)
 
     def give(dz, arr, n, dx):
-        src = pown.at[pl.ds((arr * 4 + dz) * HALF + dx * CAP, CAP), parts[n]]
-        dst = ret.at[pl.ds((arr * 2 + dx) * SLOTS + dz * CAP, CAP), parts[n]]
+        src = pown.at[pl.ds((arr * 4 + dz) * HALF + dx * CAP, CAP), parts[arr][n]]
+        dst = ret.at[pl.ds((arr * 2 + dx) * SLOTS + dz * CAP, CAP), parts[arr][n]]
         if dz == 0:
             copy = pltpu.make_async_copy(src, dst, loc_sem.at[13 + arr * 5 + n * 2 + dx])
             copy.start()
@@ -414,7 +452,6 @@
         hand[dz] = hand_over(dz)
     for dz in order:
         add_up(dz, 0, hand[dz])
-        swap(dz, 0)
         pl.semaphore_signal(credit.at[dz], inc=1, device_id=to_core, device_id_type=MESH)
 
     def backward_one(dz):
@@ -436,15 +473,19 @@
         product(dgu, wgu, dz, 1)
         hand_b[dz] = hand_over(dz)
 
+    early = len(late)
     give_back(0, 0)
-    give_back(0, 1)
-    for dz in (1, 3, 2):
-        cot_two(dz)
+    cot_two(1)
     core_wait(core_cot, 0)
     backward_one(0)
+    cot_two(3)
     backward_two(0)
+    cot_two(2)
     for dz in (1, 3, 2):
         core_wait(core_cot, dz)
+    give_back(0, 1)
+    for dz in order:
+        swap(dz, 0)
 
     near = y // 2
     other = 1 - xh
@@ -521,25 +562,32 @@
         return jnp.where(mat > 0, jnp.ones_like(mat), jnp.zeros_like(mat)) if arr else mat
 
     fins = {}
+    fin_recv = (fin_recv0, fin_recv1)
 
     def combine(arr, n):
         given(arr, n)
-        held = (tok_p, cot_p)[arr]
-        part = ret[pl.ds((arr * 2 + 1) * SLOTS, SLOTS), parts[n]]
-        held[:, parts[n]] = dot(pick(gates_p, arr), part, TN).astype(BF)
-        copy = send(held.at[:, parts[n]], fin_recv.at[arr, :, parts[n]], to_x)
+        held = (cot_p, tok_p)[arr]
+        part = ret[pl.ds((arr * 2 + 1) * SLOTS, SLOTS), parts[arr][n]]
+        held[:, parts[arr][n]] = dot(pick(gates_p, arr), part, TN).astype(BF)
+        copy = send(held.at[:, parts[arr][n]], fin_recv[arr].at[:, parts[arr][n]], to_x)
         late.append(copy)
         fins[arr, n] = copy
 
     def finish(arr, n, dst):
         if n == 2:
             given(arr, n)
-        part = ret[pl.ds(arr * 2 * SLOTS, SLOTS), parts[n]]
+        part = ret[pl.ds(arr * 2 * SLOTS, SLOTS), parts[arr][n]]
         total = dot(pick(gates, arr), part, TN)
         if n < 2:
             fins[arr, n].wait_recv()
-            total = total + fin_recv[arr, :, parts[n]].astype(F32)
-        dst[:, parts[n]] = total.astype(BF)
+            total = total + fin_recv[arr][:, parts[arr][n]].astype(F32)
+        dst[:, parts[arr][n]] = total.astype(BF)
+
+    def flush():
+        for copy in late[:early]:
+            copy.wait_send()
+            free.append(which[id(copy)])
+        del late[:early]
 
     def settle(dz):
         add_up(dz, 1, hand_b[dz])
@@ -547,59 +595,74 @@
 
     weight_grad(cots, hid, gd, other, 1 - near)
     d_a = ring_first(gd, y1d, 0, other)
+    weight_grad(cots, hid, gd, other, near)
+    flush()
+    for dz in (1, 3, 2):
+        backward_one(dz)
+    d_a = ring_second(gd, y1d, y2d, 0, other, d_a)
+    weight_grad(rows, dgu, ggu, other, 1 - near)
+    gu_a = ring_first(ggu, y1gu, 0, other)
+    weight_grad(rows, dgu, ggu, other, near)
+    settle(0)
+    backward_two(1)
+    backward_two(3)
+    settle(1)
+    backward_two(2)
+    settle(3)
+    gu_a = ring_second(ggu, y1gu, y2gu, 0, other, gu_a)
+    give_last(0)
+    settle(2)
+    give_back(1, 0)
     weight_grad(cots, hid, gd, xh, 1 - near)
     d_b = ring_first(gd, y1d, 1, xh)
-    weight_grad(cots, hid, gd, other, near)
     weight_grad(cots, hid, gd, xh, near)
-    settle(0)
-    backward_one(1)
-    backward_two(1)
-    d_a = ring_second(gd, y1d, y2d, 0, other, d_a)
-    d_b = ring_second(gd, y1d, y2d, 1, xh, d_b)
-    backward_one(3)
-    settle(1)
-    backward_two(3)
-    give_last(0)
-    backward_one(2)
-    settle(3)
-    weight_grad(rows, dgu, ggu, other, 1 - near)
-    gu_a = ring_first(ggu, y1gu, 0, other)
-    backward_two(2)
-    weight_grad(rows, dgu, ggu, other, near)
-    settle(2)
-    give_back(1, 0)
     weight_grad(rows, dgu, ggu, xh, 1 - near)
-    gu_b = ring_first(ggu, y1gu, 1, xh)
-    gu_a = ring_second(ggu, y1gu, y2gu, 0, other, gu_a)
-    d_x = ring_third(gd, y2d, xd, d_a)
-    weight_grad(rows, dgu, ggu, xh, near)
     c_tok.wait_send()
     c_cot.wait_send()
     combine(0, 0)
     combine(0, 1)
+    gu_b = ring_first(ggu, y1gu, 1, xh)
+    d_x = ring_third(gd, y2d, xd, d_a)
+    weight_grad(rows, dgu, ggu, xh, near)
     give_back(1, 1)
+    gu_x = ring_third(ggu, y2gu, xgu, gu_a)
+    d_b = ring_second(gd, y1d, y2d, 1, xh, d_b)
+    gu_b = ring_second(ggu, y1gu, y2gu, 1, xh, gu_b)
     give_last(1)
     finish(0, 2, out_ref)
-    gu_b = ring_second(ggu, y1gu, y2gu, 1, xh, gu_b)
+    stores = []
+
+    def store(src, dst):
+        copy = pltpu.make_async_copy(src, dst, loc_sem.at[23 + len(stores)])
+        copy.start()
+        stores.append(copy)
+
     ring_last(gd, y2d, xd, gd_ref, d_b, d_x)
+    store(gd_ref, gd_hbm)
     finish(0, 0, out_ref)
     finish(0, 1, out_ref)
-    gu_x = ring_third(ggu, y2gu, xgu, gu_a)
+    store(out_ref, out_hbm)
     combine(1, 0)
     combine(1, 1)
+    finish(1, 0, tgrad_ref)
+    store(tgrad_ref.at[:, parts[1][0]], tgrad_hbm.at[:, parts[1][0]])
+    ring_last(ggu, y2gu, xgu, ggu_ref, gu_b, gu_x)
+    store(ggu_ref, ggu_hbm)
     finish(1, 2, tgrad_ref)
-    finish(1, 0, tgrad_ref)
-    ring_last(ggu, y2gu, xgu, ggu_ref, gu_b, gu_x)
+    store(tgrad_ref.at[:, parts[1][2]], tgrad_hbm.at[:, parts[1][2]])
     finish(1, 1, tgrad_ref)
+    store(tgrad_ref.at[:, parts[1][1]], tgrad_hbm.at[:, parts[1][1]])
+    for copy in stores:
+        copy.wait()
 
     for copy in late:
         copy.wait_send()
     for dz in order:
         hand_b[dz].wait_send()
-    assert used[0] <= N_COPY, used[0]
-
-
-N_COPY = 200
+    assert used == [N_COPY, N_SEND], used
+
+
+N_COPY, N_SEND = 133, 88
 
 
 def exchange(ids, gates, tok, cot, proj_in, proj_out):
@@ -612,10 +675,16 @@
         jax.ShapeDtypeStruct((SH, FF), F32),
     ]
     scratch = [
+        pltpu.VMEM((TOK, D), BF),
+        pltpu.VMEM((TOK, D), BF),
+        pltpu.VMEM((SH, 2 * FF), F32),
+        pltpu.VMEM((SH, FF), F32),
+        pltpu.VMEM((2 * WIN, TOK), F32),
+        pltpu.VMEM((2 * WIN, TOK), F32),
         pltpu.VMEM((SLOTS, TOK), BF),
         pltpu.VMEM((SLOTS, TOK), BF),
         pltpu.VMEM((TOK, CA), BF),
-        pltpu.VMEM((TOK, CA), BF),
+        pltpu.VMEM((TOK, CC), BF),
         pltpu.VMEM((6 * CAP, D), BF),
         pltpu.VMEM((6 * CAP, CA), BF),
         pltpu.VMEM((ROWS, D), BF),
@@ -628,8 +697,10 @@
         pltpu.VMEM((8 * HALF, D), BF),
         pltpu.VMEM((4 * HALF, D), BF),
         pltpu.VMEM((4 * SLOTS, D), BF),
-        pltpu.VMEM((2, TOK, CA), BF),
-        pltpu.VMEM((2 * SLOTS, CB), BF),
+        pltpu.VMEM((TOK, CF), BF),
+        pltpu.VMEM((TOK, CG), BF),
+        pltpu.VMEM((SLOTS, D - CF), BF),
+        pltpu.VMEM((SLOTS, D - CG), BF),
         pltpu.VMEM((D, 2 * FF), BF),
         pltpu.VMEM((D, FF), BF),
         pltpu.VMEM((4, SH // 2, 2 * FF), BF),
@@ -638,16 +709,16 @@
         pltpu.VMEM((4, SH, FF), BF),
         pltpu.VMEM((SH, 2 * FF), BF),
         pltpu.VMEM((SH, FF), BF),
+        pltpu.SemaphoreType.DMA((N_SEND,)),
         pltpu.SemaphoreType.DMA((N_COPY,)),
-        pltpu.SemaphoreType.DMA((N_COPY,)),
-        pltpu.SemaphoreType.DMA((23,)),
+        pltpu.SemaphoreType.DMA((29,)),
         pltpu.SemaphoreType.REGULAR((4,)),
     ]
     return pl.pallas_call(
         kernel,
         out_shape=shapes,
         in_specs=[vmem] * 2 + [hbm] * 4,
-        out_specs=[vmem] * 4,
+        out_specs=[hbm] * 4,
         scratch_shapes=scratch,
         compiler_params=pltpu.CompilerParams(
             collective_id=0, has_side_effects=True, vmem_limit_bytes=64 * 2**20
@@ -659,46 +730,81 @@
     )(ids, gates, tok, cot, proj_in, proj_out)
 
 
-def adam_kernel(ggu, gd, pin, pout, first, second, out, tgrad, *outs):
-    new_in, new_out, new_first, new_second, out_copy, tgrad_copy = outs
-    out_copy[...] = out[...]
-    tgrad_copy[...] = tgrad[...]
-    for k in range(3):
-        gradient = gd[...] if k == 2 else ggu[:, k * FF : (k + 1) * FF]
-        master = pout[0] if k == 2 else pin[k, 0]
-        m = beta_one * first[k, 0] + (1.0 - beta_one) * gradient
-        v = beta_two * second[k, 0] + (1.0 - beta_two) * gradient * gradient
-        step = m / bias_one / (jnp.sqrt(v / bias_two) + adam_eps) + decay_rate * master
-        updated = master - learn_rate * step
-        new_first[k, 0] = m
-        new_second[k, 0] = v
+def adam_kernel(*refs):
+    ggu, gd, pin, pout, first, second, out, tgrad = refs[:8]
+    new_in, new_out, new_first, new_second, out_copy, tgrad_copy = refs[8:14]
+    grads, masters, firsts, seconds, held, sem = refs[14:]
+    passed = [
+        pltpu.make_async_copy(out, held.at[0], sem.at[24]),
+        pltpu.make_async_copy(tgrad, held.at[1], sem.at[25]),
+    ]
+    order = (2, 0, 1)
+    loads = {}
+    for k in order:
+        gradient = gd if k == 2 else ggu.at[:, pl.ds(k * FF, FF)]
+        master = pout.at[0] if k == 2 else pin.at[k, 0]
+        pairs = (
+            (gradient, grads.at[k]),
+            (master, masters.at[k]),
+            (first.at[k, 0], firsts.at[k]),
+            (second.at[k, 0], seconds.at[k]),
+        )
+        loads[k] = [
+            pltpu.make_async_copy(src, dst, sem.at[k * 4 + i])
+            for i, (src, dst) in enumerate(pairs)
+        ]
+        for copy in loads[k]:
+            copy.start()
+    for copy in passed:
+        copy.start()
+    stores = []
+    for k in order:
+        for copy in loads[k]:
+            copy.wait()
+
+        def tile(n, k=k):
+            at = pl.ds(pl.multiple_of(n * 16, 16), 16)
+            gradient = grads[k, at, :]
+            master = masters[k, at, :]
+            m = beta_one * firsts[k, at, :] + (1.0 - beta_one) * gradient
+            v = beta_two * seconds[k, at, :] + (1.0 - beta_two) * gradient * gradient
+            root = jnp.sqrt(v * (1.0 / bias_two)) + adam_eps
+            step = (m * (1.0 / bias_one)) / root + decay_rate * master
+            firsts[k, at, :] = m
+            seconds[k, at, :] = v
+            masters[k, at, :] = master - learn_rate * step
+
+        loop(SH // 16, tile)
+        new_master = new_out.at[0] if k == 2 else new_in.at[k, 0]
+        pairs = (
+            (masters.at[k], new_master),
+            (firsts.at[k], new_first.at[k, 0]),
+            (seconds.at[k], new_second.at[k, 0]),
+        )
+        for i, (src, dst) in enumerate(pairs):
+            copy = pltpu.make_async_copy(src, dst, sem.at[12 + k * 4 + i])
+            copy.start()
+            stores.append(copy)
         if k == 2:
-            new_out[0] = updated
-        else:
-            new_in[k, 0] = updated
+            for i, dst in enumerate((out_copy, tgrad_copy)):
+                passed[i].wait()
+                copy = pltpu.make_async_copy(held.at[i], dst, sem.at[26 + i])
+                copy.start()
+                stores.append(copy)
+    for copy in stores:
+        copy.wait()
 
 
 def adam(ggu, gd, pin, pout, first, second, out, tgrad):
-    steps = 4
-    part = SH // steps
-
-    def stacked(count):
-        return pl.BlockSpec((count, 1, part, FF), lambda i: (0, 0, i, 0))
-
-    plain = [
-        pl.BlockSpec((part, 2 * FF), lambda i: (i, 0)),
-        pl.BlockSpec((part, FF), lambda i: (i, 0)),
-    ]
-    single = pl.BlockSpec((1, part, FF), lambda i: (0, i, 0))
-    token = pl.BlockSpec((TOK // steps, D), lambda i: (i, 0))
+    hbm = pl.BlockSpec(memory_space=pl.ANY)
     arrays = (pin, pout, first, second, out, tgrad)
-    specs = [stacked(2), single, stacked(3), stacked(3), token, token]
     return pl.pallas_call(
         adam_kernel,
         out_shape=[jax.ShapeDtypeStruct(a.shape, a.dtype) for a in arrays],
-        grid=(steps,),
-        in_specs=plain + specs,
-        out_specs=specs,
+        in_specs=[hbm] * 8,
+        out_specs=[hbm] * 6,
+        scratch_shapes=[pltpu.VMEM((3, SH, FF), F32)] * 4
+        + [pltpu.VMEM((2, TOK, D), BF), pltpu.SemaphoreType.DMA((28,))],
         compiler_params=pltpu.CompilerParams(vmem_limit_bytes=64 * 2**20),
         name="adam",
     )(ggu, gd, *arrays)

time: 152 us -> 145 us (0.954)
  Pallas kernels: 150 us -> 143 us
    pallas_call x1, Pallas kernels: 143 us -> 137 us  [exchange(): pl.pallas_call(kernel, out_shape=shapes, in_specs=[vmem] * 2 + [hbm] * 4,...]
where the time goes in v4:
time: 145 us; the launch traced here: 144 us
  Pallas kernels  143 us (99%)
    pallas_call x1, Pallas kernels, exchange(): pl.pallas_call(kernel, out_shape=shapes, in_specs=[vmem] * 2 + [hbm] * 4,...  137 us
    pallas_call x1, Pallas kernels, adam(): pl.pallas_call(adam_kernel, out_shape=[jax.ShapeDtypeStruct(a.shape, a.dt...  5.74 us

profile of v4, /device:TPU:32, one launch (start us, length us, event | category | flops | bytes accessed | tf_op | source)
XLA Modules:
  0.0 143.7 jit_solution(11140181054605709595)
XLA Ops:
  0.6 137.2 %experts.1 = (bf16[128,2560]{1,0:T(8,128)(2,1)}, bf16[128,2560]{1,0:T(8,128)(2,1)}, f32[320,768]{1,0:T(8,128)}, f32[320,384]{1,0:T(8,128)}) custom-call(s32[6,128]{1,0:T(8,128)} %bitcast.2, bf16[6,128]{1,0:T(8,128)(2,1)} %bitcast.3, bf16[128,2560]{1,0:T(8,128)(2,1)} %tok_hbm.1, bf16[128,2560]{1,0:T(8,128)(2,1)} %cot_hbm.1, f32[2,1,320,384]{3,2,1,0:T(8,128)} %refs_2_.1, ...), custom_call_target="tpu_custom_call" | custom-call | flops 22649241600 | bytes 4194304 | tf_op jit(solution)/shard_map/experts/pallas_call | solution.py:717
  137.8 5.7 %adam.1 = (f32[2,1,320,384]{3,2,1,0:T(8,128)}, f32[1,320,384]{2,1,0:T(8,128)}, f32[3,1,320,384]{3,2,1,0:T(8,128)}, f32[3,1,320,384]{3,2,1,0:T(8,128)}, bf16[128,...) custom-call(f32[320,768]{1,0:T(8,128)} %get-tuple-element.16.refs_0_, f32[320,384]{1,0:T(8,128)} %get-tuple-element.17.refs_1_, ...), custom_call_target="tpu_custom_call" | custom-call | tf_op jit(solution)/shard_map/adam/pallas_call | solution.py:801

commit v5 on v4

--- a/solution.py
+++ b/solution.py
@@ -23,6 +23,7 @@
 CC = 1536
 CF = 1536
 CG = 1792
+SPLITS = (768, 1280)
 
 beta_one = 0.9
 beta_two = 0.95
@@ -285,7 +286,7 @@
     fill(gates, tok, rows, 0, 0, False, D, 512)
     z_tok0 = {dz: spread(rows, 0, 0, dz) for dz in (1, 3, 2)}
     own_in(rows, core_tok, 0)
-    c_tok = send(tok.at[:, x_first(rows)], tok_p, to_x)
+    c_tok = send(tok.at[:, x_first(rows)], tok_p.at[:, x_first(rows)], to_x)
     loads[4].wait()
     fill(gates, cot, cots, 0, 1, True, D, 512)
     gu2 = w_forward(wgu, xh, gu0)
@@ -299,13 +300,13 @@
     c_tok.wait_recv()
     for dz in (0, 1, 3, 2):
         own_on(rows, core_tok, dz)
-    fill(gates_p, tok_p, rows, 1, 0, False, CA, 896)
+    fill(gates_p, tok_p, rows, 1, 0, False, CA, CA // 2)
     z_tok1 = {dz: spread(rows, 1, 0, dz) for dz in (1, 3, 2)}
     core_tok[0, 1] = cross(rows, 0, 1, x_first(rows))
     d0 = w_first(wd)
     d_far = w_far(wd)
     gu3 = w_forward(wgu, 1 - xh, gu1)
-    c_cot = send(cot.at[:, x_first(cots)], cot_p, to_x)
+    c_cot = send(cot.at[:, x_first(cots)], cot_p.at[:, x_first(cots)], to_x)
     z_cot0[1] = spread(cots, 0, 1, 1)
     z_cot0[3] = spread(cots, 0, 1, 3)
     d2 = w_forward(wd, xh, d0)
@@ -328,8 +329,8 @@
         pre[...] = dot(rows[here, :], wgu[...], NN)
 
         def act(n):
-            src = pl.ds(pl.multiple_of(n * 16, 16), 16)
-            dst = pl.ds(pl.multiple_of(dz * SLOTS + n * 16, 16), 16)
+            src = pl.ds(pl.multiple_of(n * 32, 32), 32)
+            dst = pl.ds(pl.multiple_of(dz * SLOTS + n * 32, 32), 32)
             gate, up = pre[src, :FF], pre[src, FF:]
             sig = jax.nn.sigmoid(gate)
             active = gate * sig
@@ -337,7 +338,7 @@
             dgu[dst, :FF] = (up * (sig * (1.0 + gate * (1.0 - sig)))).astype(BF)
             dgu[dst, FF:] = active.astype(BF)
 
-        loop(SLOTS // 16, act)
+        loop(SLOTS // 32, act)
 
     def core_wait(table, dz):
         for part in range(3):
@@ -356,7 +357,7 @@
     core_wait(core_tok, 0)
     forward_one(0)
     c_cot.wait_recv()
-    fill(gates_p, cot_p, cots, 1, 1, True, CC, 768)
+    fill(gates_p, cot_p, cots, 1, 1, True, CC, CC // 2)
     z_cot1 = {dz: spread(cots, 1, 1, dz) for dz in (1, 3, 2)}
     core_cot[0, 1] = cross(cots, 0, 1, x_first(cots))
     core_wait(core_tok, 1)
@@ -400,7 +401,7 @@
         loop(HALF // 16, tile)
 
     parts = [
-        (pl.ds(0, n // 2), pl.ds(n // 2, n // 2), pl.ds(n, D - n)) for n in (CF, CG)
+        (pl.ds(0, k), pl.ds(k, n - k), pl.ds(n, D - n)) for k, n in zip(SPLITS, (CF, CG))
     ]
     xrets = (xret0, xret1)
 
@@ -459,13 +460,13 @@
         pre[:, :FF] = dot(cots[here, :], wd[...], NN)
 
         def act(n):
-            src = pl.ds(pl.multiple_of(n * 16, 16), 16)
-            dst = pl.ds(pl.multiple_of(dz * SLOTS + n * 16, 16), 16)
+            src = pl.ds(pl.multiple_of(n * 32, 32), 32)
+            dst = pl.ds(pl.multiple_of(dz * SLOTS + n * 32, 32), 32)
             dh = pre[src, :FF]
             dgu[dst, :FF] = (dgu[dst, :FF].astype(F32) * dh).astype(BF)
             dgu[dst, FF:] = (dgu[dst, FF:].astype(F32) * dh).astype(BF)
 
-        loop(SLOTS // 16, act)
+        loop(SLOTS // 32, act)
 
     def backward_two(dz):
         hand[dz].wait_send()
@@ -683,8 +684,8 @@
         pltpu.VMEM((2 * WIN, TOK), F32),
         pltpu.VMEM((SLOTS, TOK), BF),
         pltpu.VMEM((SLOTS, TOK), BF),
-        pltpu.VMEM((TOK, CA), BF),
-        pltpu.VMEM((TOK, CC), BF),
+        pltpu.VMEM((TOK, max(CA, CG)), BF),
+        pltpu.VMEM((TOK, max(CC, CF)), BF),
         pltpu.VMEM((6 * CAP, D), BF),
         pltpu.VMEM((6 * CAP, CA), BF),
         pltpu.VMEM((ROWS, D), BF),
@@ -763,7 +764,7 @@
             copy.wait()
 
         def tile(n, k=k):
-            at = pl.ds(pl.multiple_of(n * 16, 16), 16)
+            at = pl.ds(pl.multiple_of(n * 80, 16), 80)
             gradient = grads[k, at, :]
             master = masters[k, at, :]
             m = beta_one * firsts[k, at, :] + (1.0 - beta_one) * gradient
@@ -774,7 +775,7 @@
             seconds[k, at, :] = v
             masters[k, at, :] = master - learn_rate * step
 
-        loop(SH // 16, tile)
+        loop(SH // 80, tile)
         new_master = new_out.at[0] if k == 2 else new_in.at[k, 0]
         pairs = (
             (masters.at[k], new_master),

time: 145 us -> 145 us (level)
  no operation moved by 1% of the time
where the time goes in v5:
time: 145 us; the launch traced here: 143 us
  Pallas kernels  143 us (99%)
    pallas_call x1, Pallas kernels, exchange(): pl.pallas_call(kernel, out_shape=shapes, in_specs=[vmem] * 2 + [hbm] * 4,...  137 us
    pallas_call x1, Pallas kernels, adam(): pl.pallas_call(adam_kernel, out_shape=[jax.ShapeDtypeStruct(a.shape, a.dt...  5.74 us

profile of v5, /device:TPU:32, one launch (start us, length us, event | category | flops | bytes accessed | tf_op | source)
XLA Modules:
  0.0 143.4 jit_solution(17097092633606314457)
XLA Ops:
  0.6 136.9 %experts.1 = (bf16[128,2560]{1,0:T(8,128)(2,1)}, bf16[128,2560]{1,0:T(8,128)(2,1)}, f32[320,768]{1,0:T(8,128)}, f32[320,384]{1,0:T(8,128)}) custom-call(s32[6,128]{1,0:T(8,128)} %bitcast.2, bf16[6,128]{1,0:T(8,128)(2,1)} %bitcast.3, bf16[128,2560]{1,0:T(8,128)(2,1)} %tok_hbm.1, bf16[128,2560]{1,0:T(8,128)(2,1)} %cot_hbm.1, f32[2,1,320,384]{3,2,1,0:T(8,128)} %refs_2_.1, ...), custom_call_target="tpu_custom_call" | custom-call | flops 22649241600 | bytes 4194304 | tf_op jit(solution)/shard_map/experts/pallas_call | solution.py:718
  137.5 5.7 %adam.1 = (f32[2,1,320,384]{3,2,1,0:T(8,128)}, f32[1,320,384]{2,1,0:T(8,128)}, f32[3,1,320,384]{3,2,1,0:T(8,128)}, f32[3,1,320,384]{3,2,1,0:T(8,128)}, bf16[128,...) custom-call(f32[320,768]{1,0:T(8,128)} %get-tuple-element.16.refs_0_, f32[320,384]{1,0:T(8,128)} %get-tuple-element.17.refs_1_, ...), custom_call_target="tpu_custom_call" | custom-call | tf_op jit(solution)/shard_map/adam/pallas_call | solution.py:802
